TPU v7x, 128 devices: a whole 4x4x4 slice. The times are simulated.
128 devices in a mesh: dp: 4 (over y), pipe: 4 (over z_hi, core), tensor: 8 (over z_lo, x).
Axes of the slice: x: 4, y: 4, z: 4 (z_hi: 2, z_lo: 2; z = z_hi * 2 + z_lo), core: 2. Of those that a mesh axis runs over, the one named last changes fastest.
Arguments:
- lm_inputs: bfloat16 [4, 4, 96, 8192], P('dp', 'pipe'), may hold values from -180 to 180
- top_grad: bfloat16 [4, 2, 96, 8192], P('dp', None, 'tensor'), may hold values from -6 to 6
- phase_gain: float32 [2, 8192], replicated, may hold values from 0.5 to 2
- query_weight: bfloat16 [4, 8192, 8, 256], P('pipe', None, 'tensor'), may hold values from -1.08275726 to 1.08275726
- kv_weight: bfloat16 [4, 8192, 8, 128], P('pipe', None, 'tensor'), may hold values from -0.06629126 to 0.06629126
- out_weight: bfloat16 [4, 8, 256, 8192], P('pipe', 'tensor'), may hold values from -0.09375 to 0.09375
- segment_ids: int32 [4, 2, 96], P('dp'), may hold values from 0 to 3, never falling along the last dimension, each value on 1 to 48 neighbouring positions
- visual_pos: int32 [4, 96], P('dp'), may hold values from 0 to 191, as said below
- patches: bfloat16 [4, 96, 5120], P('dp', 'pipe'), may hold values from -6 to 6
- ln_gain: float32 [1280], replicated, may hold values from 0.5 to 2
- ln_bias: float32 [1280], replicated, may hold values from -3 to 3
- fc1_weight: bfloat16 [5120, 2560], P(None, 'tensor'), may hold values from -0.078125 to 0.078125
- fc1_bias: float32 [2560], P('tensor'), may hold values from -3 to 3
- fc2_weight: bfloat16 [2560, 8192], P('tensor'), may hold values from -0.125 to 0.125
Outputs:
- patch_grads: bfloat16 [4, 96, 5120], P('dp', 'pipe')
- fc1_grad: float32 [5120, 2560], P(('dp', 'pipe'), 'tensor')
- fc2_grad_t: float32 [8192, 2560], P(('dp', 'pipe'), 'tensor')
Inputs may be any that keep to these rules, and one draw needn't show every extreme that they name: `visual_pos`: sorted increasing and distinct; they come in runs of 4 rows starting at multiples of 4, and micro-batch m holds exactly 48 of them, all in rows m * 96 to (m + 1) * 96 - 1. `segment_ids`: numbers never fall along a micro-batch.
All inputs are finite; a program needn't handle non-finite values.
Results may differ from a plain program's by a relative error of at most 0.027.
Values may be sent and summed in bfloat16 or wider, within the bound.
A program may use at most 128 MiB of HBM per device.

v0:
```python
import jax
import jax.numpy as jnp
from jax import lax
from jax.sharding import PartitionSpec as P

EPS_RMS = 1e-06
EPS_LN = 1e-06
THETA = 1000000.0


def swapped(block, axis, stride):
    count = lax.axis_size(axis)
    route = []
    for low in range(count):
        high = low | 1 << stride
        if high != low and high < count:
            route += [(low, high), (high, low)]
    return lax.ppermute(block, axis, route)


def shifted(block, axis, distance):
    devices = range(lax.axis_size(axis))
    route = [(i - distance, i) for i in devices if i - distance in devices]
    return lax.ppermute(block, axis, route)


def rope_tables(length, head_dim):
    half_dim = head_dim // 2
    freq_table = THETA ** (-(2.0 * jnp.arange(half_dim, dtype=jnp.float32)) / head_dim)
    angles = jnp.arange(length, dtype=jnp.float32)[:, None] * freq_table[None, :]
    return (jnp.cos(angles), jnp.sin(angles))


def rotate(vectors, cosine, sine_table, direction):
    half_dim = vectors.shape[-1] // 2
    first_half = vectors[..., :half_dim]
    second_half = vectors[..., half_dim:]
    return jnp.concatenate(
        [
            first_half * cosine - direction * second_half * sine_table,
            second_half * cosine + direction * first_half * sine_table,
        ],
        axis=-1,
    )


def gelu_slope(values):
    normal_cdf = 0.5 * (1.0 + jax.scipy.special.erf(values * 0.7071067811865476))
    density = jnp.exp(-0.5 * values * values) * 0.3989422804014327
    return normal_cdf + values * density


def select_by(flag, first_value, second_value):
    return jnp.where(flag, first_value, second_value)


def contract_last(left_side, right_side):
    return lax.dot_general(
        left_side, right_side, (((1,), (1,)), ((), ())), preferred_element_type=jnp.float32
    )


def contract_first(left_side, right_side):
    return lax.dot_general(
        left_side, right_side, (((0,), (0,)), ((), ())), preferred_element_type=jnp.float32
    )


def phase_step(
    inputs, incoming_rows, norm_gain, query_w, kv_w, out_w, segments, half_index, tensor_index
):
    length, model_width = inputs.shape
    row_count = incoming_rows.shape[0]
    incoming = lax.all_gather(incoming_rows, "tensor", axis=0, tiled=True)
    heads_kv = kv_w.shape[1]
    head_dim = kv_w.shape[2]
    half_dim = head_dim // 2
    per_half = query_w.shape[2] // head_dim
    values_in = inputs.astype(jnp.float32)
    scale_rms = lax.rsqrt(jnp.mean(values_in * values_in, axis=-1, keepdims=True) + EPS_RMS)
    unit_vals = values_in * scale_rms
    normed = (unit_vals * norm_gain[None, :]).astype(jnp.bfloat16)
    cosine, sine_table = rope_tables(length, head_dim)
    query_flat = query_w.reshape(model_width, -1)
    kv_flat = kv_w.reshape(model_width, -1)
    query_rows = jnp.dot(normed, query_flat, preferred_element_type=jnp.float32).reshape(
        length, heads_kv, per_half, head_dim
    )
    queries = rotate(
        query_rows, cosine[:, None, None, :], sine_table[:, None, None, :], 1.0
    ).astype(jnp.bfloat16)
    kv_own = (
        jnp.dot(normed, kv_flat, preferred_element_type=jnp.float32)
        .reshape(length, heads_kv, head_dim)
        .astype(jnp.bfloat16)
    )
    kv_other = swapped(kv_own, "pipe", 0)
    is_first = half_index == 0
    kv_lower = select_by(is_first, kv_own, kv_other)
    kv_upper = select_by(is_first, kv_other, kv_own)
    key_heads = jnp.concatenate([kv_lower[..., :half_dim], kv_upper[..., :half_dim]], axis=-1)
    value_heads = jnp.concatenate([kv_lower[..., half_dim:], kv_upper[..., half_dim:]], axis=-1)
    key_heads = rotate(
        key_heads.astype(jnp.float32), cosine[:, None, :], sine_table[:, None, :], 1.0
    ).astype(jnp.bfloat16)
    grad_out = (
        contract_last(incoming, out_w.reshape(-1, model_width))
        .reshape(length, heads_kv, per_half, head_dim)
        .astype(jnp.bfloat16)
    )
    factor = head_dim ** (-0.5)
    scores = (
        jnp.einsum("sghe,tge->ghst", queries, key_heads, preferred_element_type=jnp.float32)
        * factor
    )
    positions = jnp.arange(length)
    allowed = (positions[None, :] <= positions[:, None]) & (segments[:, None] == segments[None, :])
    scores = jnp.where(allowed, scores, -1e30)
    top_score = jnp.max(scores, axis=-1, keepdims=True)
    weights = jnp.where(allowed, jnp.exp(scores - top_score), 0.0)
    probs_full = weights / jnp.sum(weights, axis=-1, keepdims=True)
    probs_low = probs_full.astype(jnp.bfloat16)
    grad_prob = jnp.einsum(
        "sghe,tge->ghst", grad_out, value_heads, preferred_element_type=jnp.float32
    )
    delta_rows = jnp.sum(probs_full * grad_prob, axis=-1, keepdims=True)
    grad_score = (probs_full * (grad_prob - delta_rows) * factor).astype(jnp.bfloat16)
    grad_query = jnp.einsum(
        "ghst,tge->sghe", grad_score, key_heads, preferred_element_type=jnp.float32
    )
    grad_query = rotate(
        grad_query, cosine[:, None, None, :], sine_table[:, None, None, :], -1.0
    ).astype(jnp.bfloat16)
    grad_key = jnp.einsum("ghst,sghe->tge", grad_score, queries, preferred_element_type=jnp.float32)
    grad_key = rotate(grad_key, cosine[:, None, :], sine_table[:, None, :], -1.0)
    grad_value = jnp.einsum(
        "ghst,sghe->tge", probs_low, grad_out, preferred_element_type=jnp.float32
    )
    key_lower = grad_key[..., :half_dim]
    key_upper = grad_key[..., half_dim:]
    value_lower = grad_value[..., :half_dim]
    value_upper = grad_value[..., half_dim:]
    own_share = jnp.concatenate(
        [select_by(is_first, key_lower, key_upper), select_by(is_first, value_lower, value_upper)],
        axis=-1,
    )
    peer_share = jnp.concatenate(
        [select_by(is_first, key_upper, key_lower), select_by(is_first, value_upper, value_lower)],
        axis=-1,
    )
    received = swapped(peer_share.astype(jnp.bfloat16), "pipe", 0).astype(peer_share.dtype)
    grad_kv = (own_share + received).astype(jnp.bfloat16)
    query_grads = grad_query.reshape(length, -1)
    kv_grads_flat = grad_kv.reshape(length, -1)
    partial_sum = lax.psum_scatter(
        (contract_last(query_grads, query_flat) + contract_last(kv_grads_flat, kv_flat)).astype(
            jnp.bfloat16
        ),
        "tensor",
        scatter_dimension=0,
        tiled=True,
    ).astype(jnp.float32)
    partner_sum = swapped(partial_sum.astype(jnp.bfloat16), "pipe", 0).astype(partial_sum.dtype)
    grad_normed = partial_sum + partner_sum
    block_start = tensor_index * row_count
    unit_rows = lax.dynamic_slice_in_dim(unit_vals, block_start, row_count, 0)
    scale_rows = lax.dynamic_slice_in_dim(scale_rms, block_start, row_count, 0)
    grad_unit = grad_normed * norm_gain[None, :]
    inner_mean = jnp.mean(grad_unit * unit_rows, axis=-1, keepdims=True)
    grad_norm = scale_rows * (grad_unit - unit_rows * inner_mean)
    return (incoming_rows.astype(jnp.float32) + grad_norm).astype(jnp.bfloat16)


def local(
    lm_inputs,
    top_grad,
    phase_gain,
    query_weight,
    kv_weight,
    out_weight,
    segment_ids,
    visual_pos,
    patches,
    ln_gain,
    ln_bias,
    fc1_weight,
    fc1_bias,
    fc2_weight,
):
    pipe_index = lax.axis_index("pipe")
    tensor_index = lax.axis_index("tensor")
    phase_index = pipe_index // 2
    half_index = pipe_index % 2
    is_first = half_index == 0
    norm_gain = lax.dynamic_index_in_dim(phase_gain, phase_index, 0, keepdims=False)
    query_w = query_weight[0]
    kv_w = kv_weight[0]
    out_w = out_weight[0]
    own_inputs = lm_inputs[0, 0]
    other_inputs = swapped(own_inputs, "pipe", 0)
    inputs_first = select_by(is_first, own_inputs, other_inputs)
    inputs_second = select_by(is_first, other_inputs, own_inputs)
    segments_first = segment_ids[0, 0]
    segments_second = segment_ids[0, 1]
    upper_first = top_grad[0, 0]
    upper_second = top_grad[0, 1]

    def run_phase(inputs, incoming_rows, segments):
        return phase_step(
            inputs,
            incoming_rows,
            norm_gain,
            query_w,
            kv_w,
            out_w,
            segments,
            half_index,
            tensor_index,
        )

    def send_down(phase_rows):
        return shifted(phase_rows, "pipe", -2)

    upper_out_first = run_phase(inputs_first, upper_first, segments_first)
    upper_out_second = run_phase(inputs_second, upper_second, segments_second)
    lower_first = run_phase(inputs_first, send_down(upper_out_first), segments_first)
    lower_second = run_phase(inputs_second, send_down(upper_out_second), segments_second)
    row_count = upper_first.shape[0]
    seq_length = own_inputs.shape[0]
    model_width = own_inputs.shape[1]
    owner_rows = patches.shape[1]
    owner_count = lax.axis_size("pipe")
    slot_count = min(row_count, owner_rows)
    positions = visual_pos[0]
    token_total = positions.shape[0]
    sender_rows = select_by(is_first, lower_first, lower_second)
    shard_start = half_index * seq_length + tensor_index * row_count
    first_token = jnp.sum(positions < shard_start)
    end_token = jnp.sum(positions < shard_start + row_count)
    owner_ids = jnp.arange(owner_count, dtype=jnp.int32)[:, None]
    slot_ids = jnp.arange(slot_count, dtype=jnp.int32)[None, :]
    token_ids = jnp.maximum(first_token, owner_ids * owner_rows) + slot_ids
    valid_slot = token_ids < jnp.minimum(end_token, (owner_ids + 1) * owner_rows)
    local_rows = jnp.take(positions, jnp.clip(token_ids, 0, token_total - 1)) - shard_start
    local_rows = jnp.clip(local_rows, 0, row_count - 1)
    outgoing = jnp.where(
        valid_slot[..., None],
        jnp.take(sender_rows, local_rows, axis=0),
        jnp.zeros((), jnp.bfloat16),
    )
    arrived = lax.all_to_all(outgoing, "pipe", split_axis=0, concat_axis=0, tiled=True)
    own_tokens = pipe_index * owner_rows + jnp.arange(owner_rows, dtype=jnp.int32)
    own_positions = lax.dynamic_slice_in_dim(positions, pipe_index * owner_rows, owner_rows, 0)
    sender_ids = own_positions // seq_length
    block_start = own_positions // row_count * row_count
    block_first = jnp.sum(positions[None, :] < block_start[:, None], axis=1)
    slot_index = own_tokens - jnp.maximum(block_first, pipe_index * owner_rows)
    from_here = own_positions % seq_length // row_count == tensor_index
    flat_index = sender_ids * slot_count + jnp.clip(slot_index, 0, slot_count - 1)
    placed = jnp.take(arrived.reshape(-1, model_width), flat_index, axis=0)
    placed = jnp.where(from_here[:, None], placed, jnp.zeros((), jnp.bfloat16))
    rows_grad = lax.psum(placed.astype(jnp.float32).astype(jnp.bfloat16), "tensor")
    context = ln_gain.shape[0]
    patch_vals = patches[0].astype(jnp.float32).reshape(owner_rows, -1, context)
    centered = patch_vals - jnp.mean(patch_vals, axis=-1, keepdims=True)
    inv_std = lax.rsqrt(jnp.mean(centered * centered, axis=-1, keepdims=True) + EPS_LN)
    patch_unit = centered * inv_std
    merger_normed = (patch_unit * ln_gain + ln_bias).astype(jnp.bfloat16).reshape(owner_rows, -1)
    hidden_pre = (
        jnp.dot(merger_normed, fc1_weight, preferred_element_type=jnp.float32) + fc1_bias[None, :]
    )
    activated = jax.nn.gelu(hidden_pre, approximate=False).astype(jnp.bfloat16)
    grad_act = contract_last(rows_grad, fc2_weight)
    grad_pre = (grad_act * gelu_slope(hidden_pre)).astype(jnp.bfloat16)
    grad_merged = lax.psum(
        contract_last(grad_pre, fc1_weight).astype(jnp.bfloat16), "tensor"
    ).astype(jnp.float32)
    patch_grad_unit = grad_merged.reshape(owner_rows, -1, context) * ln_gain
    patch_grad = inv_std * (
        patch_grad_unit
        - jnp.mean(patch_grad_unit, axis=-1, keepdims=True)
        - patch_unit * jnp.mean(patch_grad_unit * patch_unit, axis=-1, keepdims=True)
    )
    patch_grad = patch_grad.reshape(owner_rows, -1).astype(jnp.bfloat16)
    fc1_term = contract_first(merger_normed, grad_pre)
    fc2_term = contract_first(rows_grad, activated)
    fc1_grad, fc2_grad = (
        lax.psum_scatter(
            fc1_term.astype(jnp.bfloat16), ("dp", "pipe"), scatter_dimension=0, tiled=True
        ).astype(jnp.float32),
        lax.psum_scatter(
            fc2_term.astype(jnp.bfloat16), ("dp", "pipe"), scatter_dimension=0, tiled=True
        ).astype(jnp.float32),
    )
    return (patch_grad[None], fc1_grad, fc2_grad)


def solution(mesh):
    in_specs = (
        P("dp", "pipe", None, None),
        P("dp", None, "tensor", None),
        P(),
        P("pipe", None, "tensor", None),
        P("pipe", None, "tensor", None),
        P("pipe", "tensor", None, None),
        P("dp", None, None),
        P("dp", None),
        P("dp", "pipe", None),
        P(),
        P(),
        P(None, "tensor"),
        P("tensor"),
        P("tensor", None),
    )
    out_specs = (P("dp", "pipe", None), P(("dp", "pipe"), "tensor"), P(("dp", "pipe"), "tensor"))
    return jax.shard_map(local, mesh=mesh, in_specs=in_specs, out_specs=out_specs, check_vma=False)
```

profile of v0, /device:TPU:1, one launch (start us, length us, event | category | flops | bytes accessed | tf_op | source)
XLA Modules:
  0.0 796.5 jit_solution(14575112727366217829)
XLA Ops:
  7.2 3.7 fusion.219
  12.6 6.4 copy.83
  20.6 2.8 fusion.17
  23.5 2.4 convert_multiply_fusion
  26.5 3.9 copy-done.9
  40.0 15.8 %all-gather.11.cloned.1.call-done = bf16[1,1,96,8192]{3,1,0,2:T(2,128)(2,1)} async-done(((bf16[1,1,12,8192]{3,1,0,2:T(2,128)(2,1)}), bf16[1,1,96,8192]{3,1,0,2:T(2,128)(2,1)}) %all-gather.11.cloned.1.call-update) | async-done | bytes 1572880 | tf_op jit(solution)/shard_map/all_gather | solution.py:74
  55.8 5.5 fusion.47
  67.1 35.0 %all-gather.9.cloned.1.call-done = bf16[1,1,96,8192]{3,1,0,2:T(2,128)(2,1)} async-done(((bf16[1,1,12,8192]{3,1,0,2:T(2,128)(2,1)}), bf16[1,1,96,8192]{3,1,0,2:T(2,128)(2,1)}) %all-gather.9.cloned.1.call-update) | async-done | bytes 1572880 | tf_op jit(solution)/shard_map/all_gather | solution.py:74
  102.2 5.6 fusion.44
  109.6 3.3 collective-permute-start.8
  116.8 2.0 fusion.6
  118.8 2.0 fusion.4
  120.8 52.2 %fusion.218 = (bf16[16,8192]{1,0:T(8,128)(2,1)}, bf16[16,8192]{1,0:T(8,128)(2,1)}) fusion(bf16[96,8192]{1,0:T(8,128)(2,1)} %fusion.4, bf16[96,8192]{1,0:T(8,128)(2,1)} %fusion.6), kind=kCustom, calls=%all-reduce-scatter.5 | all-reduce-scatter fusion | flops 2097153 | bytes 3670528
  173.0 2.3 collective-permute-start.13
  177.1 2.0 collective-permute-start.14
  182.0 5.8 collective-permute-start.17
  187.9 2.2 collective-permute-start.18
  190.1 10.0 %concatenate.224 = bf16[44,8192]{1,0:T(8,128)(2,1)} concatenate(bf16[12,8192]{1,0:T(8,128)(2,1)} %collective-permute-done.14, bf16[16,8192]{1,0:T(8,128)(2,1)} %collective-permute-done.13, bf16[16,8192]{1,0:T(8,128)(2,1)} %get-tuple-element.19), dimensions={0} | concatenate | bytes 1441792
  201.8 2.2 collective-permute-start.3
  204.0 10.0 %concatenate.226 = bf16[44,8192]{1,0:T(8,128)(2,1)} concatenate(bf16[12,8192]{1,0:T(8,128)(2,1)} %collective-permute-done.18, bf16[16,8192]{1,0:T(8,128)(2,1)} %collective-permute-done.17, bf16[16,8192]{1,0:T(8,128)(2,1)} %get-tuple-element.20), dimensions={0} | concatenate | bytes 1441792
  217.7 2.2 multiply_reduce_fusion.1
  219.9 3.4 fusion.65
  224.6 10.0 %collective-permute-done.10 = bf16[12,8192]{1,0:T(8,128)(2,1)} collective-permute-done((bf16[12,8192]{1,0:T(8,128)(2,1)S(1)}, bf16[12,8192]{1,0:T(8,128)(2,1)}, u32[]{:S(2)}, u32[]{:S(2)}) %collective-permute-start.10) | collective-permute-done | bytes 196640 | tf_op jit(solution)/shard_map/ppermute | solution.py:24
  236.0 9.3 %collective-permute-done.4 = bf16[12,8192]{1,0:T(8,128)(2,1)} collective-permute-done((bf16[12,8192]{1,0:T(8,128)(2,1)}, bf16[12,8192]{1,0:T(8,128)(2,1)}, u32[]{:S(2)}, u32[]{:S(2)}) %collective-permute-start.4) | collective-permute-done | bytes 196640 | tf_op jit(solution)/shard_map/ppermute | solution.py:24
  245.9 1.9 multiply_minimum_fusion
  254.5 2.0 reshape.1108
  256.5 1.8 reduce_sum.187
  262.7 5.6 all-gather.15.cloned.1.call-done
  268.3 2.7 reshape.1160
  271.0 4.1 convolution_convert_fusion.3
  277.4 33.8 %all-gather.13.cloned.1.call-done = bf16[8,12,8192]{2,1,0:T(8,128)(2,1)} async-done(((bf16[1,12,8192]{2,1,0:T(8,128)(2,1)}), bf16[8,12,8192]{2,1,0:T(8,128)(2,1)}) %all-gather.13.cloned.1.call-update) | async-done | bytes 1572880 | tf_op jit(solution)/shard_map/all_gather | solution.py:74
  311.2 2.6 reshape.1151
  314.0 4.2 convolution_convert_fusion.4
  320.2 5.4 collective-permute-start.11
  329.2 2.0 fusion.7
  331.2 2.0 fusion.5
  333.2 52.2 %fusion.217 = (bf16[16,8192]{1,0:T(8,128)(2,1)}, bf16[16,8192]{1,0:T(8,128)(2,1)}) fusion(bf16[96,8192]{1,0:T(8,128)(2,1)} %fusion.5, bf16[96,8192]{1,0:T(8,128)(2,1)} %fusion.7), kind=kCustom, calls=%all-reduce-scatter.4 | all-reduce-scatter fusion | flops 2097153 | bytes 3670528
  385.4 2.0 collective-permute-start.19
  393.0 6.2 collective-permute-start.15
  399.2 2.7 collective-permute-start.16
  402.6 10.0 %concatenate.227 = bf16[44,8192]{1,0:T(8,128)(2,1)} concatenate(bf16[12,8192]{1,0:T(8,128)(2,1)} %copy-done.47, bf16[16,8192]{1,0:T(8,128)(2,1)} %collective-permute-done.19, bf16[16,8192]{1,0:T(8,128)(2,1)} %get-tuple-element.16), dimensions={0} | concatenate | bytes 1441792
  412.6 1.8 constant_dynamic-slice_fusion
  414.4 2.2 collective-permute-start.12
  416.5 10.0 %concatenate.225 = bf16[44,8192]{1,0:T(8,128)(2,1)} concatenate(bf16[12,8192]{1,0:T(8,128)(2,1)} %collective-permute-done.16, bf16[16,8192]{1,0:T(8,128)(2,1)} %collective-permute-done.15, bf16[16,8192]{1,0:T(8,128)(2,1)} %get-tuple-element.15), dimensions={0} | concatenate | bytes 1441792
  429.3 2.2 multiply_reduce_fusion.2
  431.5 2.4 fusion.68
  433.9 1.9 gather_fusion.1
  435.8 2.3 reshape.1119
  438.2 2.4 select_select_fusion
  440.6 4.5 all-to-all-start
  449.2 11.1 %all-to-all-done = bf16[4,12,8192]{2,1,0:T(8,128)(2,1)} async-done(((bf16[4,12,8192]{2,1,0:T(8,128)(2,1)}), bf16[4,12,8192]{2,1,0:T(8,128)(2,1)}, u32[]{:S(2)}, u32[]{:S(2)}) %all-to-all-start) | async-done | bytes 786464 | tf_op jit(solution)/shard_map/all_to_all | solution.py:251
  460.3 2.3 reshape.1106
  462.6 3.2 gather_fusion.2
  465.8 1.9 select_select_fusion.1
  469.8 2.3 convolution_add_fusion.4
  472.1 62.4 %all-reduce.13.cloned.1.call-done = bf16[24,8192]{1,0:T(8,128)(2,1)} async-done(((bf16[24,8192]{1,0:T(8,128)(2,1)}), bf16[24,8192]{1,0:T(8,128)(2,1)}) %all-reduce.13.cloned.1.call-update) | async-done | bytes 393232 | tf_op jit(solution)/shard_map/psum | solution.py:262
  534.5 4.0 fusion.58
  540.6 4.2 convolution_convert_fusion.1
  544.8 4.9 convolution_convert_fusion
  549.7 64.4 %all-reduce.15.cloned.1.call-done = bf16[24,5120]{1,0:T(8,128)(2,1)} async-done(((bf16[24,5120]{1,0:T(8,128)(2,1)}), bf16[24,5120]{1,0:T(8,128)(2,1)}) %all-reduce.15.cloned.1.call-update) | async-done | bytes 245776 | tf_op jit(solution)/shard_map/psum | solution.py:275
  614.1 2.0 reshape.1107
  619.1 80.6 %reduce-scatter.11.cloned.1.call-done = bf16[320,320]{1,0:T(8,128)(2,1)} async-done(((bf16[5120,320]{1,0:T(8,128)(2,1)}), bf16[320,320]{1,0:T(8,128)(2,1)}) %reduce-scatter.11.cloned.1.call-update) | async-done | bytes 204816 | tf_op jit(solution)/shard_map/reduce_scatter | solution.py:288
  701.5 86.1 %reduce-scatter.13.cloned.1.call-done = bf16[512,320]{0,1:T(8,128)(2,1)} async-done(((bf16[8192,320]{0,1:T(8,128)(2,1)}), bf16[512,320]{0,1:T(8,128)(2,1)}) %reduce-scatter.13.cloned.1.call-update) | async-done | bytes 327696 | tf_op jit(solution)/shard_map/reduce_scatter | solution.py:291
  787.5 1.9 convert_element_type.450
  (360 shorter events, 78.2 us)
Async XLA Ops:
  7.2 462.6 %copy-start = (bf16[5120,320]{0,1:T(8,128)(2,1)S(1)}, bf16[5120,320]{0,1:T(8,128)(2,1)}, u32[]{:S(2)}) copy-start(bf16[5120,320]{0,1:T(8,128)(2,1)} %param.25) | copy-start | bytes 9830404
  7.2 48.6 %all-gather.11.cloned.1.call-start = ((), (), s32[]{:S(2)}) async-start(), calls=%async_computation.8 | async-start | bytes 3538944 | tf_op jit(solution)/shard_map/all_gather | solution.py:74
  10.9 91.2 %all-gather.9.cloned.1.call-start = ((), (), s32[]{:S(2)}) async-start(), calls=%async_computation.7 | async-start | bytes 3538944 | tf_op jit(solution)/shard_map/all_gather | solution.py:74
  11.0 9.7 %collective-permute-start = (bf16[96,8192]{1,0:T(8,128)(2,1)}, bf16[96,8192]{1,0:T(8,128)(2,1)}, u32[]{:S(2)}, u32[]{:S(2)}) collective-permute-start(bf16[96,8192]{1,0:T(8,128)(2,1)} %bitcast.402), channel_id=1, source_target_pairs={{0,8},{8,0},{16,24},{24,16},{1,9},{9,1},{17,25},{25,17},{2,10},{10... | collective-permute-start | bytes 4718600 | tf_op jit(solution)/shard_map/ppermute | solution.py:18
  12.5 255.8 %all-gather.15.cloned.1.call-start = ((), (), s32[]{:S(2)}) async-start(), calls=%async_computation.10 | async-start | bytes 2359296 | tf_op jit(solution)/shard_map/all_gather | solution.py:74
  12.6 102.0 %copy-start.69 = (f32[64]{0:T(128)}, f32[64]{0:T(128)S(1)}, u32[]{:S(2)}) copy-start(f32[64]{0:T(128)S(1)} %multiply_power_fusion) | copy-start | bytes 772
  12.6 8.0 %copy-start.68 = (f32[2,8192]{1,0:T(2,128)S(1)}, f32[2,8192]{1,0:T(2,128)}, u32[]{:S(2)}) copy-start(f32[2,8192]{1,0:T(2,128)} %param.16) | copy-start | bytes 196612
  20.6 14.5 %copy-start.28 = (f32[96,64]{1,0:T(8,128)}, f32[96,64]{1,0:T(8,128)S(1)}, u32[]{:S(2)}) copy-start(f32[96,64]{1,0:T(8,128)S(1)} %get-tuple-element.83) | copy-start | bytes 73732
  20.6 408.6 %copy-start.13 = (f32[1,8192]{1,0:T(1,128)}, f32[1,8192]{1,0:T(1,128)S(1)}, u32[]{:S(2)}) copy-start(f32[1,8192]{1,0:T(1,128)S(1)} %constant_dynamic-slice_fusion.4) | copy-start | bytes 98308
  33.9 2.0 collective-permute-start.7
  34.6 3.0 collective-permute-start.1
  35.8 26.7 %copy-start.18 = (bf16[96,2,64]{2,0,1:T(8,128)(2,1)}, bf16[96,2,64]{2,0,1:T(8,128)(2,1)S(1)}, u32[]{:S(2)}) copy-start(bf16[96,2,64]{2,0,1:T(8,128)(2,1)S(1)} %get-tuple-element.35) | copy-start | bytes 73732
  35.9 26.7 %copy-start.20 = (bf16[96,2,64]{2,0,1:T(8,128)(2,1)}, bf16[96,2,64]{2,0,1:T(8,128)(2,1)S(1)}, u32[]{:S(2)}) copy-start(bf16[96,2,64]{2,0,1:T(8,128)(2,1)S(1)} %get-tuple-element.36) | copy-start | bytes 73732
  40.0 21.6 %copy-start.71 = (f32[2,96]{1,0:T(2,128)}, f32[2,96]{1,0:T(2,128)S(1)}, u32[]{:S(2)}) copy-start(f32[2,96]{1,0:T(2,128)S(1)} %fusion.73) | copy-start | bytes 2308
  55.8 7.8 copy-start.22
  55.8 7.8 copy-start.25
  63.9 45.4 %copy-start.66 = (f32[2,96]{1,0:T(2,128)}, f32[2,96]{1,0:T(2,128)S(1)}, u32[]{:S(2)}) copy-start(f32[2,96]{1,0:T(2,128)S(1)} %get-tuple-element.88) | copy-start | bytes 2308
  102.2 10.7 %copy-start.17 = (f32[96,1,2,128]{3,0,2,1:T(8,128)S(1)}, f32[96,1,2,128]{3,0,2,1:T(8,128)}, u32[]{:S(2)}) copy-start(f32[96,1,2,128]{3,0,2,1:T(8,128)} %convolution_bitcast_fusion.2) | copy-start | bytes 294916
  102.2 10.7 %copy-start.29 = (f32[96,64]{1,0:T(8,128)S(1)}, f32[96,64]{1,0:T(8,128)}, u32[]{:S(2)}) copy-start(f32[96,64]{1,0:T(8,128)} %copy-done.28) | copy-start | bytes 73732
  102.2 10.7 %copy-start.33 = (f32[96,64]{1,0:T(8,128)S(1)}, f32[96,64]{1,0:T(8,128)}, u32[]{:S(2)}) copy-start(f32[96,64]{1,0:T(8,128)} %get-tuple-element.81) | copy-start | bytes 73732
  102.2 11.0 %copy-start.2 = (bf16[1,8192,1,256]{3,1,2,0:T(8,128)(2,1)S(1)}, bf16[1,8192,1,256]{3,1,2,0:T(8,128)(2,1)}, u32[]{:S(2)}) copy-start(bf16[1,8192,1,256]{3,1,2,0:T(8,128)(2,1)} %param.17) | copy-start | bytes 12582916
  109.6 7.1 collective-permute-start.8
  115.0 3.8 collective-permute-start.2
  120.8 58.3 %copy-start.93 = (u32[128]{0:T(128)S(1)}, u32[128]{0:T(128)}, u32[]{:S(2)}) copy-start(u32[128]{0:T(128)} %constant.223) | copy-start | bytes 1540
  173.0 17.0 %collective-permute-start.13 = (bf16[16,8192]{1,0:T(8,128)(2,1)}, bf16[16,8192]{1,0:T(8,128)(2,1)}, u32[]{:S(2)}, u32[]{:S(2)}) collective-permute-start(bf16[16,8192]{1,0:T(8,128)(2,1)} %get-tuple-element.19), channel_id=1, source_target_pairs={{0,1},{1,2},{2,3},{3,4},{4,5},{5,6},{6,7},{8,9},{9,10},{10,11},{11... | collective-permute-start | bytes 786440
  177.1 13.0 %collective-permute-start.14 = (bf16[12,8192]{1,0:T(8,128)(2,1)}, bf16[12,8192]{1,0:T(8,128)(2,1)}, u32[]{:S(2)}, u32[]{:S(2)}) collective-permute-start(bf16[12,8192]{1,0:T(8,128)(2,1)} %slice.238), channel_id=1, source_target_pairs={{0,2},{1,3},{2,4},{3,5},{4,6},{5,7},{8,10},{9,11},{10,12},{11,13},... | collective-permute-start | bytes 589832
  182.0 22.0 %collective-permute-start.17 = (bf16[16,8192]{1,0:T(8,128)(2,1)}, bf16[16,8192]{1,0:T(8,128)(2,1)}, u32[]{:S(2)}, u32[]{:S(2)}) collective-permute-start(bf16[16,8192]{1,0:T(8,128)(2,1)} %get-tuple-element.20), channel_id=1, source_target_pairs={{0,1},{1,2},{2,3},{3,4},{4,5},{5,6},{6,7},{8,9},{9,10},{10,11},{11... | collective-permute-start | bytes 786440
  187.9 16.1 %collective-permute-start.18 = (bf16[12,8192]{1,0:T(8,128)(2,1)}, bf16[12,8192]{1,0:T(8,128)(2,1)}, u32[]{:S(2)}, u32[]{:S(2)}) collective-permute-start(bf16[12,8192]{1,0:T(8,128)(2,1)} %slice.240), channel_id=1, source_target_pairs={{0,2},{1,3},{2,4},{3,5},{4,6},{5,7},{8,10},{9,11},{10,12},{11,13},... | collective-permute-start | bytes 589832
  201.8 15.4 %collective-permute-start.3 = (bf16[12,8192]{1,0:T(8,128)(2,1)}, bf16[12,8192]{1,0:T(8,128)(2,1)}, u32[]{:S(2)}, u32[]{:S(2)}) collective-permute-start(bf16[12,8192]{1,0:T(8,128)(2,1)} %constant_dynamic-slice_fusion.3), channel_id=1, source_target_pairs={{0,8},{8,0},{16,24},{24,16},{1,9},{9,1},{17,25},{25,17},{2,10},{10... | collective-permute-start | bytes 589832 | tf_op jit(solution)/shard_map/ppermute | solution.py:18
  215.8 29.5 %copy-start.1 = (s32[1,96]{1,0:T(1,128)S(1)}, s32[1,96]{1,0:T(1,128)}, u32[]{:S(2)}) copy-start(s32[1,96]{1,0:T(1,128)} %param.21) | copy-start | bytes 1156
  215.8 1.9 collective-permute-start.9
  216.5 31.3 %copy-start.82 = (f32[12]{0:T(128)}, f32[12]{0:T(128)S(1)}, u32[]{:S(2)}) copy-start(f32[12]{0:T(128)S(1)} %dynamic-slice.7) | copy-start | bytes 148
  217.2 17.4 %copy-start.84 = (f32[12]{0:T(128)}, f32[12]{0:T(128)S(1)}, u32[]{:S(2)}) copy-start(f32[12]{0:T(128)S(1)} %dynamic-slice.8) | copy-start | bytes 148
  223.3 11.3 %collective-permute-start.10 = (bf16[12,8192]{1,0:T(8,128)(2,1)S(1)}, bf16[12,8192]{1,0:T(8,128)(2,1)}, u32[]{:S(2)}, u32[]{:S(2)}) collective-permute-start(bf16[12,8192]{1,0:T(8,128)(2,1)S(1)} %get-tuple-element.63), channel_id=1, source_target_pairs={{16,0},{24,8},{17,1},{25,9},{18,2},{26,10},{19,3},{27,11},{20,4},{... | collective-permute-start | bytes 589832 | tf_op jit(solution)/shard_map/ppermute | solution.py:24
  234.6 76.6 %all-gather.13.cloned.1.call-start = ((), (), s32[]{:S(2)}) async-start(), calls=%async_computation.9 | async-start | bytes 2359296 | tf_op jit(solution)/shard_map/all_gather | solution.py:74
  234.7 10.6 %collective-permute-start.4 = (bf16[12,8192]{1,0:T(8,128)(2,1)}, bf16[12,8192]{1,0:T(8,128)(2,1)}, u32[]{:S(2)}, u32[]{:S(2)}) collective-permute-start(bf16[12,8192]{1,0:T(8,128)(2,1)} %get-tuple-element.64), channel_id=1, source_target_pairs={{16,0},{24,8},{17,1},{25,9},{18,2},{26,10},{19,3},{27,11},{20,4},{... | collective-permute-start | bytes 589832 | tf_op jit(solution)/shard_map/ppermute | solution.py:24
  314.0 11.7 %copy-start.30 = (f32[96,64]{1,0:T(8,128)S(1)}, f32[96,64]{1,0:T(8,128)}, u32[]{:S(2)}) copy-start(f32[96,64]{1,0:T(8,128)} %copy-done.28) | copy-start | bytes 73732
  314.0 11.7 %copy-start.34 = (f32[96,64]{1,0:T(8,128)S(1)}, f32[96,64]{1,0:T(8,128)}, u32[]{:S(2)}) copy-start(f32[96,64]{1,0:T(8,128)} %get-tuple-element.81) | copy-start | bytes 73732
  314.0 11.9 %copy-start.3 = (bf16[1,8192,1,256]{3,1,2,0:T(8,128)(2,1)S(1)}, bf16[1,8192,1,256]{3,1,2,0:T(8,128)(2,1)}, u32[]{:S(2)}) copy-start(bf16[1,8192,1,256]{3,1,2,0:T(8,128)(2,1)} %param.17) | copy-start | bytes 12582916
  320.2 8.9 %collective-permute-start.11 = (bf16[96,1,128]{2,0,1:T(8,128)(2,1)S(1)}, bf16[96,1,128]{2,0,1:T(8,128)(2,1)S(1)}, u32[]{:S(2)}, u32[]{:S(2)}) collective-permute-start(bf16[96,1,128]{2,0,1:T(8,128)(2,1)S(1)} %pad_maximum_fusion.9), channel_id=1, source_target_pairs={{0,8},{8,0},{16,24},{24,16},{1,9},{9,1},{17,25},{25,17},{2,10},{10... | collective-permute-start | bytes 73736 | tf_op jit(solution)/shard_map/ppermute | solution.py:18
  327.5 3.7 collective-permute-start.5
  333.2 57.4 %copy-start.79 = (s32[4]{0:T(128)S(1)}, s32[4]{0:T(128)}, u32[]{:S(2)}) copy-start(s32[4]{0:T(128)} %copy-done.78) | copy-start | bytes 52
  333.2 57.4 %copy-start.86 = (s32[4]{0:T(128)S(1)}, s32[4]{0:T(128)}, u32[]{:S(2)}) copy-start(s32[4]{0:T(128)} %get-tuple-element.100) | copy-start | bytes 52
  385.4 17.2 %collective-permute-start.19 = (bf16[16,8192]{1,0:T(8,128)(2,1)}, bf16[16,8192]{1,0:T(8,128)(2,1)}, u32[]{:S(2)}, u32[]{:S(2)}) collective-permute-start(bf16[16,8192]{1,0:T(8,128)(2,1)} %get-tuple-element.16), channel_id=1, source_target_pairs={{0,1},{1,2},{2,3},{3,4},{4,5},{5,6},{6,7},{8,9},{9,10},{10,11},{11... | collective-permute-start | bytes 786440
  388.0 43.4 %copy-start.80 = (s32[1,24]{1,0:T(1,128)}, s32[1,24]{1,0:T(1,128)S(1)}, u32[]{:S(2)}) copy-start(s32[1,24]{1,0:T(1,128)S(1)} %get-tuple-element.22) | copy-start | bytes 292
  389.1 12.8 %collective-permute-start.20 = (bf16[12,8192]{1,0:T(8,128)(2,1)S(1)}, bf16[12,8192]{1,0:T(8,128)(2,1)S(1)}, u32[]{:S(2)}, u32[]{:S(2)}) collective-permute-start(bf16[12,8192]{1,0:T(8,128)(2,1)S(1)} %slice.241), channel_id=1, source_target_pairs={{0,2},{1,3},{2,4},{3,5},{4,6},{5,7},{8,10},{9,11},{10,12},{11,13},... | collective-permute-start | bytes 589832
  393.0 38.5 %copy-start.83 = (f32[12]{0:T(128)S(1)}, f32[12]{0:T(128)}, u32[]{:S(2)}) copy-start(f32[12]{0:T(128)} %copy-done.82) | copy-start | bytes 148
  393.0 38.5 %copy-start.85 = (f32[12]{0:T(128)S(1)}, f32[12]{0:T(128)}, u32[]{:S(2)}) copy-start(f32[12]{0:T(128)} %copy-done.84) | copy-start | bytes 148
  393.0 23.6 %collective-permute-start.15 = (bf16[16,8192]{1,0:T(8,128)(2,1)}, bf16[16,8192]{1,0:T(8,128)(2,1)}, u32[]{:S(2)}, u32[]{:S(2)}) collective-permute-start(bf16[16,8192]{1,0:T(8,128)(2,1)} %get-tuple-element.15), channel_id=1, source_target_pairs={{0,1},{1,2},{2,3},{3,4},{4,5},{5,6},{6,7},{8,9},{9,10},{10,11},{11... | collective-permute-start | bytes 786440
  399.2 17.4 %collective-permute-start.16 = (bf16[12,8192]{1,0:T(8,128)(2,1)}, bf16[12,8192]{1,0:T(8,128)(2,1)}, u32[]{:S(2)}, u32[]{:S(2)}) collective-permute-start(bf16[12,8192]{1,0:T(8,128)(2,1)} %slice.239), channel_id=1, source_target_pairs={{0,2},{1,3},{2,4},{3,5},{4,6},{5,7},{8,10},{9,11},{10,12},{11,13},... | collective-permute-start | bytes 589832
  414.4 13.9 %collective-permute-start.12 = (bf16[12,8192]{1,0:T(8,128)(2,1)}, bf16[12,8192]{1,0:T(8,128)(2,1)}, u32[]{:S(2)}, u32[]{:S(2)}) collective-permute-start(bf16[12,8192]{1,0:T(8,128)(2,1)} %constant_dynamic-slice_fusion), channel_id=1, source_target_pairs={{0,8},{8,0},{16,24},{24,16},{1,9},{9,1},{17,25},{25,17},{2,10},{10... | collective-permute-start | bytes 589832 | tf_op jit(solution)/shard_map/ppermute | solution.py:18
  427.6 1.6 collective-permute-start.6
  435.8 9.3 %copy-start.94 = (s32[24]{0:T(128)S(1)}, s32[24]{0:T(128)}, u32[]{:S(2)}) copy-start(s32[24]{0:T(128)} %fusion.174) | copy-start | bytes 292
  435.8 9.5 %copy-start.53 = (f32[24,4]{1,0:T(8,128)S(1)}, f32[24,4]{1,0:T(8,128)}, u32[]{:S(2)}) copy-start(f32[24,4]{1,0:T(8,128)} %add_rsqrt_fusion) | copy-start | bytes 1156
  438.1 8.1 %copy-start.51 = (f32[24,4]{1,0:T(8,128)S(1)}, f32[24,4]{1,0:T(8,128)}, u32[]{:S(2)}) copy-start(f32[24,4]{1,0:T(8,128)} %copy-done.50) | copy-start | bytes 1156
  438.1 9.1 %copy-start.57 = (f32[1280]{0:T(1024)S(1)}, f32[1280]{0:T(1024)}, u32[]{:S(2)}) copy-start(f32[1280]{0:T(1024)} %param.23) | copy-start | bytes 15364
  438.1 9.2 %copy-start.77 = (f32[1280]{0:T(1024)S(1)}, f32[1280]{0:T(1024)}, u32[]{:S(2)}) copy-start(f32[1280]{0:T(1024)} %param.24) | copy-start | bytes 15364
  438.2 9.8 %copy-start.81 = (s32[1,24]{1,0:T(1,128)S(1)}, s32[1,24]{1,0:T(1,128)}, u32[]{:S(2)}) copy-start(s32[1,24]{1,0:T(1,128)} %copy-done.80) | copy-start | bytes 292
  440.6 19.7 %all-to-all-start = ((bf16[4,12,8192]{2,1,0:T(8,128)(2,1)}), bf16[4,12,8192]{2,1,0:T(8,128)(2,1)}, u32[]{:S(2)}, u32[]{:S(2)}) async-start(bf16[4,12,8192]{2,1,0:T(8,128)(2,1)} %select_select_fusion), calls=%async_computation | async-start | bytes 2097152 | tf_op jit(solution)/shard_map/all_to_all | solution.py:251
  445.1 89.4 %all-reduce.13.cloned.1.call-start = ((), (), s32[]{:S(2)}) async-start(), calls=%async_computation.3 | async-start | bytes 786432 | tf_op jit(solution)/shard_map/psum | solution.py:262
  449.2 18.6 %copy-start.14 = (bf16[1,24,5120]{2,1,0:T(8,128)(2,1)S(1)}, bf16[1,24,5120]{2,1,0:T(8,128)(2,1)}, u32[]{:S(2)}) copy-start(bf16[1,24,5120]{2,1,0:T(8,128)(2,1)} %param.22) | copy-start | bytes 737284
  467.7 146.4 %all-reduce.15.cloned.1.call-start = ((), (), s32[]{:S(2)}) async-start(), calls=%async_computation.4 | async-start | bytes 491520 | tf_op jit(solution)/shard_map/psum | solution.py:275
  540.5 159.2 %reduce-scatter.11.cloned.1.call-start = ((), (), s32[]{:S(2)}) async-start(), calls=%async_computation.5 | async-start | bytes 4177920 | tf_op jit(solution)/shard_map/reduce_scatter | solution.py:288
  544.7 242.8 %reduce-scatter.13.cloned.1.call-start = ((), (), s32[]{:S(2)}) async-start(), calls=%async_computation.6 | async-start | bytes 5570560 | tf_op jit(solution)/shard_map/reduce_scatter | solution.py:291
  (61 other events, 268.5 us)
Sparse Core Ops, SparseCore 0:
  11.0 44.6 all-gather.10
  58.0 44.0 all-gather.8
  234.7 33.5 all-gather.14
  269.8 41.3 all-gather.12
  467.8 66.6 all-reduce.12
  540.6 73.4 all-reduce.14
  618.2 81.4 reduce-scatter.10
  703.8 83.6 reduce-scatter.12
where the time goes:
time: 806 us; the launch traced here: 796 us
  waiting for transfers between devices  416 us (52%)
  blocking collectives  104 us (13%)
  local copies, waits for them, and re-layouts  101 us (13%)
  matrix products  61.7 us (8%)
  other arithmetic  49.2 us (6%)
  starting transfers between devices  48 us (6%)
  between operations  16.4 us (2%)
    unnamed x2, blocking collectives  104 us
    all_gather x4, waiting for transfers between devices, phase_step(): incoming = lax.all_gather(incoming_rows, 'tensor', axis=0, tiled=True)  90.2 us
    reduce_scatter x1, waiting for transfers between devices, local(): lax.psum_scatter(fc2_term.astype(jnp.bfloat16), ('dp', 'pipe'), scatter_d...  86.1 us
    reduce_scatter x1, waiting for transfers between devices, local(): lax.psum_scatter(fc1_term.astype(jnp.bfloat16), ('dp', 'pipe'), scatter_d...  80.6 us
    unnamed x209, local copies, waits for them, and re-layouts  68.3 us
    psum x1, waiting for transfers between devices, local(): lax.psum(contract_last(grad_pre, fc1_weight).astype(jnp.bfloat16), 'tensor')  64.4 us
    psum x1, waiting for transfers between devices, local(): lax.psum(placed.astype(jnp.float32).astype(jnp.bfloat16), 'tensor')  62.4 us
    dot_general x14, matrix products, contract_last(): lax.dot_general(left_side, right_side, (((1,), (1,)), ((), ())), preferre...  38.3 us
  transfers between devices with their start and end apart: 30, of which 13 were waited for; matrix products, arithmetic and copies ran while one was open for 19% of the time, Pallas kernels for 0%

commit v1 on v0

v1 whole, which is shorter than its diff:
```python
import functools

import jax
import jax.numpy as jnp
import numpy as np
from jax import lax
from jax.experimental import pallas as pl
from jax.experimental.pallas import tpu as pltpu
from jax.sharding import PartitionSpec as P

EPS_RMS = 1e-06
EPS_LN = 1e-06
THETA = 1000000.0
MESH = pl.DeviceIdType.MESH
F32 = jnp.float32
BF16 = jnp.bfloat16
SEQ = 96
WIDTH = 8192
HALF = 4096
BLK = 512
HEAD = 128
FACTOR = HEAD**-0.5
VIS = 48
CTX = 1280
PIECE = 320
LANES = 384


def nn(a, b):
    return lax.dot_general(a, b, (((1,), (0,)), ((), ())), preferred_element_type=F32)


def nt(a, b):
    return lax.dot_general(a, b, (((1,), (1,)), ((), ())), preferred_element_type=F32)


def tn(a, b):
    return lax.dot_general(a, b, (((0,), (0,)), ((), ())), preferred_element_type=F32)


def each(count, body):
    def step(i, carry):
        body(i)
        return carry

    lax.fori_loop(0, count, step, 0)


def eye_mask(size):
    return lax.broadcasted_iota(jnp.int32, (size, size), 0) == lax.broadcasted_iota(
        jnp.int32, (size, size), 1
    )


def to_row(column):
    size = column.shape[0]
    return jnp.sum(jnp.where(eye_mask(size), column, 0.0), axis=0, keepdims=True)


def to_column(row):
    size = row.shape[1]
    return jnp.sum(jnp.where(eye_mask(size), row, 0.0), axis=1, keepdims=True)


class Sems:
    def __init__(self):
        self.numbers = {}

    def __call__(self, *name):
        return self.numbers.setdefault(name, len(self.numbers))


def kernel(
    x_hbm,
    tg_hbm,
    gain_ref,
    wq_hbm,
    wkv_hbm,
    wo_hbm,
    seg_ref,
    pos_ref,
    patches_ref,
    lng_ref,
    lnb_ref,
    fc1_hbm,
    fc1b_ref,
    fc2_hbm,
    cos_ref,
    sin_ref,
    tgsel_ref,
    pg_out,
    fc1_out,
    fc2_out,
    w3,
    wo,
    f1,
    f2,
    xo,
    xb,
    sc,
    gb,
    tg,
    inc,
    own_p,
    other_p,
    pf,
    qs,
    ks,
    vs,
    probs,
    gx_own,
    gx_other,
    acts,
    ins,
    inr,
    part,
    r1,
    r2,
    r3_send,
    r3,
    xsum,
    out_block,
    vis,
    pu,
    iv,
    mn,
    mns,
    act,
    slope,
    nblk,
    lgb,
    ga_own,
    ga_other,
    gpre,
    mnr,
    actr,
    gpr,
    visr,
    pgp,
    pgpr,
    pgs,
    pgr,
    send_sem,
    recv_sem,
    local_sem,
):
    dp = lax.axis_index("dp")
    pipe = lax.axis_index("pipe")
    ten = lax.axis_index("tensor")
    phase = pipe // 2
    core = pipe % 2
    zl = ten // 4
    xx = ten % 4
    sems = Sems()
    locals_ = Sems()

    def device(s=None, b=None, z=None, x=None, d=None, t=None):
        s = phase if s is None else s
        b = core if b is None else b
        if t is None:
            t = (zl if z is None else z) * 4 + (xx if x is None else x)
        return (dp if d is None else d, 2 * s + b, t)

    sibling = device(b=1 - core)
    right_x = lax.rem(xx + 1, 4)
    left_x = lax.rem(xx + 3, 4)
    far_x = lax.rem(xx + 2, 4)
    right = device(x=right_x)
    left = device(x=left_x)
    zmate = device(z=1 - zl)
    cross = device(s=1 - phase, z=1 - zl)

    barrier = pltpu.get_barrier_semaphore()
    count = 0
    for o in range(1, 16):
        code = lax.rem(core * 8 + ten + o, 16)
        pl.semaphore_signal(
            barrier, inc=1, device_id=device(b=code // 8, t=lax.rem(code, 8)), device_id_type=MESH
        )
        code = lax.rem(dp * 4 + pipe + o, 16)
        pl.semaphore_signal(
            barrier, inc=1, device_id=(code // 4, lax.rem(code, 4), ten), device_id_type=MESH
        )
        count += 2
    pl.semaphore_signal(barrier, inc=1, device_id=cross, device_id_type=MESH)
    count += 1

    def local(name, src, dst):
        copy = pltpu.make_async_copy(src, dst, local_sem.at[locals_(name)])
        copy.start()
        return copy

    def remote(name, src, dst, to):
        number = sems(*name)
        copy = pltpu.make_async_remote_copy(
            src_ref=src,
            dst_ref=dst,
            send_sem=send_sem.at[number],
            recv_sem=recv_sem.at[number],
            device_id=to,
            device_id_type=MESH,
        )
        copy.start()
        return copy

    def arrive(name, ref):
        pltpu.make_async_copy(ref, ref, recv_sem.at[sems(*name)]).wait()

    mine = core * HALF
    theirs = (1 - core) * HALF
    lx = local("x", x_hbm, xo)
    lxh = local("xh", x_hbm.at[:, pl.ds(mine, HALF)], xb.at[core])
    lq = local("q", wq_hbm.at[pl.ds(mine, HALF), :], w3.at[core])
    lkv = local(
        "kv", wkv_hbm.at[pl.ds(mine, HALF), :], w3.at[2, :, pl.ds(core * HEAD, HEAD)]
    )
    lo = local("o", wo_hbm.at[:, pl.ds(mine, HALF)], wo.at[pl.ds(core * 256, 256), :])
    lf1 = local("f1", fc1_hbm, f1)
    lf2 = local("f2", fc2_hbm.at[:, pl.ds(mine, HALF)], f2)

    pl.semaphore_wait(barrier, count)

    class Gather:
        def __init__(self, name, ref, width, hz):
            self.name, self.ref, self.width = name, ref, width
            self.slots = {
                "h": hz * 4 + xx,
                "hr": hz * 4 + right_x,
                "hl": hz * 4 + left_x,
                "hf": hz * 4 + far_x,
                "k": (1 - hz) * 4 + xx,
                "kr": (1 - hz) * 4 + right_x,
                "kl": (1 - hz) * 4 + left_x,
                "kf": (1 - hz) * 4 + far_x,
            }
            self.sent = []

        def view(self, slot, part_):
            ref = self.ref.at[self.slots[slot]]
            if part_ is not None:
                ref = ref.at[:, pl.ds(part_ * (self.width // 2), self.width // 2)]
            return ref

        def send(self, tag, slot, to, part_=None):
            ref = self.view(slot, part_)
            self.sent.append((sems(self.name, tag), ref))
            remote((self.name, tag), ref, ref, to)

        def got(self, tag, slot, part_=None):
            arrive((self.name, tag), self.view(slot, part_))

        def start(self):
            self.sent = []
            self.send("r1", "h", right)
            self.send("l1", "h", left)
            self.send("z", "h", zmate)

        def second(self):
            self.got("z", "k")
            self.send("r2", "k", right)
            self.send("l2", "k", left)

        def third(self):
            self.got("r1", "hl")
            self.send("fr1", "hl", right, 0)
            self.got("l1", "hr")
            self.send("fl1", "hr", left, 1)

        def fourth(self):
            self.got("r2", "kl")
            self.send("fr2", "kl", right, 0)
            self.got("l2", "kr")
            self.send("fl2", "kr", left, 1)

        def last(self):
            self.got("fr1", "hf", 0)
            self.got("fl1", "hf", 1)
            self.got("fr2", "kf", 0)
            self.got("fl2", "kf", 1)

        def rest(self):
            self.second()
            self.third()
            self.fourth()
            self.last()

        def drain(self):
            for number, ref in self.sent:
                pltpu.make_async_copy(ref, ref, send_sem.at[number]).wait()

    class Scatter:
        def __init__(self, m, rows):
            self.m, self.rows, self.sent = m, rows, []

        def block(self, z, x, cols=None):
            cols = slice(None) if cols is None else pl.ds(cols * 256, 256)
            return part.at[self.m, z * 4 + x, pl.ds(0, self.rows), cols]

        def one(self, side, z):
            return r1.at[self.m, side, z, pl.ds(0, self.rows), :]

        def two(self, side, z):
            return r2.at[self.m, side, z, pl.ds(0, self.rows), :]

        def three(self, ref):
            return ref.at[self.m, pl.ds(0, self.rows), :]

        def first(self, z):
            self.sent.append(
                remote(("s1r", self.m, z), self.block(z, far_x, 0), self.one(0, z), right)
            )
            self.sent.append(
                remote(("s1l", self.m, z), self.block(z, far_x, 1), self.one(1, z), left)
            )

        def second(self, z):
            arrive(("s1r", self.m, z), self.one(0, z))
            ref = self.block(z, right_x, 0)
            ref[...] = (ref[...].astype(F32) + self.one(0, z)[...].astype(F32)).astype(BF16)
            self.sent.append(
                remote(("s2r", self.m, z), self.block(z, right_x), self.two(0, z), right)
            )
            arrive(("s1l", self.m, z), self.one(1, z))
            ref = self.block(z, left_x, 1)
            ref[...] = (ref[...].astype(F32) + self.one(1, z)[...].astype(F32)).astype(BF16)
            self.sent.append(
                remote(("s2l", self.m, z), self.block(z, left_x), self.two(1, z), left)
            )

        def total(self, z):
            return (
                self.block(z, xx)[...].astype(F32)
                + self.two(0, z)[...].astype(F32)
                + self.two(1, z)[...].astype(F32)
            )

        def third(self):
            for z in range(2):
                arrive(("s2r", self.m, z), self.two(0, z))
                arrive(("s2l", self.m, z), self.two(1, z))
            self.three(r3_send)[...] = self.total(1 - zl).astype(BF16)
            self.sent.append(
                remote(("s3", self.m), self.three(r3_send), self.three(r3), zmate)
            )
            self.three(xsum)[...] = self.total(zl)

        def result(self):
            arrive(("s3", self.m), self.three(r3))
            return self.three(xsum)[...] + self.three(r3)[...].astype(F32)

        def drain(self):
            for copy in self.sent:
                copy.wait_send()

    sent = []
    tg_gathers = {m: Gather(("tg", m), tg.at[m], 1024, zl) for m in range(2)}
    upper = phase == 1

    @pl.when(upper)
    def _():
        for m in (1, 0):
            copy = local(("tg", m), tg_hbm.at[m, core], tg.at[m, ten])
            copy.wait()
            tg_gathers[m].start()

    sent.append(remote(("x",), x_hbm.at[:, pl.ds(theirs, HALF)], xb.at[core], sibling))
    sent.append(remote(("wq",), wq_hbm.at[pl.ds(theirs, HALF), :], w3.at[core], sibling))
    sent.append(
        remote(
            ("wkv",),
            wkv_hbm.at[pl.ds(theirs, HALF), :],
            w3.at[2, :, pl.ds(core * HEAD, HEAD)],
            sibling,
        )
    )
    sent.append(
        remote(
            ("wo",),
            wo_hbm.at[:, pl.ds(theirs, HALF)],
            wo.at[pl.ds(core * 256, 256), :],
            sibling,
        )
    )

    for i in range(8):
        pair = gain_ref[:, pl.ds(pl.multiple_of(mine + i * BLK, BLK), BLK)]
        gb[i] = jnp.where(upper, pair[1:2, :], pair[0:1, :])

    lx.wait()
    acc = jnp.zeros((SEQ, 1), F32)

    def square(i, acc):
        v = xo[:, pl.ds(pl.multiple_of(i * 1024, 1024), 1024)].astype(F32)
        return acc + jnp.sum(v * v, axis=1, keepdims=True)

    acc = lax.fori_loop(0, 8, square, acc)
    sc[core] = jnp.broadcast_to(lax.rsqrt(acc / WIDTH + EPS_RMS), (SEQ, HEAD))
    sent.append(remote(("sc",), sc.at[core], sc.at[core], sibling))

    for q in range(4):
        v = patches_ref[:, q * CTX : (q + 1) * CTX].astype(F32)
        v = v - jnp.mean(v, axis=1, keepdims=True)
        inv = lax.rsqrt(jnp.mean(v * v, axis=1, keepdims=True) + EPS_LN)
        pu[core, q] = v * inv
        iv[core, q] = jnp.broadcast_to(inv, (24, HEAD))
    sent.append(remote(("pu",), pu.at[core], pu.at[core], sibling))
    sent.append(remote(("iv",), iv.at[core], iv.at[core], sibling))

    @pl.when(upper)
    def _():
        for m in (1, 0):
            tg_gathers[m].second()
            tg_gathers[m].third()

    lxh.wait()
    lq.wait()
    lkv.wait()
    arrive(("x",), xb.at[1 - core])
    arrive(("sc",), sc.at[1 - core])
    arrive(("wq",), w3.at[1 - core])
    arrive(("wkv",), w3.at[2, :, pl.ds((1 - core) * HEAD, HEAD)])
    own_p[...] = jnp.zeros_like(own_p)

    def project(i):
        cols = pl.ds(pl.multiple_of(i * BLK, BLK), BLK)
        rows = [
            (xb[m, :, cols].astype(F32) * sc[m][:, 0:1] * gb[i]).astype(BF16) for m in range(2)
        ]
        normed = jnp.concatenate(rows, axis=0)
        for j in range(3):
            own_p[:, j * 256 : (j + 1) * 256] += nn(normed, w3[j, cols, :])

    each(8, project)
    sent.append(remote(("p",), own_p, other_p, sibling))

    @pl.when(upper)
    def _():
        for m in (1, 0):
            tg_gathers[m].fourth()

    arrive(("p",), other_p)
    pf[...] = own_p[...] + other_p[...]

    lane = lax.broadcasted_iota(jnp.int32, (SEQ, HEAD), 1)
    low = lane < 64

    def rope(v, direction):
        return v * cos_ref[...] + direction * pltpu.roll(v, 64, 1) * sin_ref[...]

    def stacked(v):
        return jnp.concatenate([v[:, h * HEAD : (h + 1) * HEAD] for h in range(4)], axis=0)

    def forward(m):
        rows = pf[m * SEQ : (m + 1) * SEQ, :]
        q = jnp.concatenate(
            [rope(rows[:, h * HEAD : (h + 1) * HEAD], 1.0) for h in range(4)], axis=0
        ).astype(BF16)
        kv0 = rows[:, 512:640].astype(BF16).astype(F32)
        kv1 = rows[:, 640:768].astype(BF16).astype(F32)
        k = rope(jnp.where(low, kv0, pltpu.roll(kv1, 64, 1)), 1.0).astype(BF16)
        v = jnp.where(low, pltpu.roll(kv0, 64, 1), kv1).astype(BF16)
        qs[m] = q
        ks[m] = k
        vs[m] = v
        scores = nt(q, k) * FACTOR
        seg = seg_ref[m : m + 1, :].astype(F32)
        seg_col = to_column(seg)
        index_row = lax.broadcasted_iota(jnp.int32, (SEQ, SEQ), 0)
        index_col = lax.broadcasted_iota(jnp.int32, (SEQ, SEQ), 1)
        allowed = jnp.where((index_col <= index_row) & (seg_col == seg), 1.0, 0.0)
        allowed = jnp.concatenate([allowed] * 4, axis=0) > 0.5
        scores = jnp.where(allowed, scores, -1e30)
        top = jnp.max(scores, axis=1, keepdims=True)
        weights = jnp.where(allowed, jnp.exp(scores - top), 0.0)
        probs[m] = weights / jnp.sum(weights, axis=1, keepdims=True)

    for m in (1, 0):
        forward(m)

    def head_grads(m):
        gx_own[m] = jnp.zeros((SEQ, 512), F32)

        def step(i):
            cols = pl.ds(pl.multiple_of(i * BLK, BLK), BLK)
            gx_own[m] += nt(inc[m, i], wo[:, cols])

        each(8, step)
        return remote(("gx", m), gx_own.at[m], gx_other.at[m], sibling)

    def backward(m):
        arrive(("gx", m), gx_other.at[m])
        go = stacked(gx_own[m] + gx_other[m]).astype(BF16)
        pr = probs[m]
        gp = nt(go, vs[m])
        delta = jnp.sum(pr * gp, axis=1, keepdims=True)
        gs = (pr * (gp - delta) * FACTOR).astype(BF16)
        gq = nn(gs, ks[m])
        gk = rope(tn(gs, qs[m]), -1.0)
        gv = tn(pr.astype(BF16), go)
        pieces = [rope(gq[h * SEQ : (h + 1) * SEQ, :], -1.0) for h in range(4)]
        pieces.append(jnp.where(low, gk, pltpu.roll(gv, 64, 1)))
        pieces.append(jnp.where(low, pltpu.roll(gk, 64, 1), gv))
        inner = jnp.zeros((SEQ, 1), F32)
        for h in range(6):
            low_piece = pieces[h].astype(BF16)
            acts[m, :, h * HEAD : (h + 1) * HEAD] = low_piece
            inner += jnp.sum(
                low_piece.astype(F32) * pf[m * SEQ : (m + 1) * SEQ, h * HEAD : (h + 1) * HEAD],
                axis=1,
                keepdims=True,
            )
        row = to_row(inner / WIDTH)
        ins[m, :, 0:SEQ] = jnp.broadcast_to(row, (8, SEQ))
        out = []
        for o in range(1, 8):
            to = lax.rem(ten + o, 8)
            out.append(remote(("in", m, o), ins.at[m], inr.at[m, ten], device(t=to)))
        return out

    def inner_row(m):
        total = ins[m, 0:1, 0:SEQ]
        for o in range(1, 8):
            src = lax.rem(ten + 8 - o, 8)
            arrive(("in", m, o), inr.at[m, src])
            total += inr[m, src, 0:1, 0:SEQ]
        return total

    def back_project(m, z, x, left_side):
        i = z * 4 + x
        rows = pl.ds(pl.multiple_of(i * BLK, BLK), BLK)
        acc = nt(left_side[:, 0:256], w3[0, rows, :])
        acc += nt(left_side[:, 256:512], w3[1, rows, :])
        acc += nt(left_side[:, 512:768], w3[2, rows, :])
        part[m, i, pl.ds(0, left_side.shape[0]), :] = acc.astype(BF16)

    def scatter_first(m, rows, left_side):
        s = Scatter(m, rows)
        for z in range(2):
            back_project(m, z, far_x, left_side)
            s.first(z)
        for x in (right_x, left_x, xx):
            for z in range(2):
                back_project(m, z, x, left_side)
        return s

    def merger_forward():
        lf1.wait()
        lf2.wait()
        arrive(("pu",), pu.at[1 - core])
        arrive(("iv",), iv.at[1 - core])
        gain = lng_ref[...]
        bias = lnb_ref[...]
        hidden = jnp.zeros((VIS, PIECE), F32)
        for q in range(4):
            n = jnp.concatenate([pu[0, q], pu[1, q]], axis=0)
            low_n = (n * gain + bias).astype(BF16)
            mn[:, q * CTX : (q + 1) * CTX] = low_n
            for j in range(4):
                mns[q * 4 + j, :, 0:PIECE] = low_n[:, j * PIECE : (j + 1) * PIECE]
            hidden += nt(low_n, f1[:, q * CTX : (q + 1) * CTX])
            lgb[q] = gain[:, q * PIECE : (q + 1) * PIECE]
        for q in range(2):
            n = jnp.concatenate([pu[0, 2 * core + q], pu[1, 2 * core + q]], axis=0)
            for j in range(4):
                nblk[q * 4 + j] = n[:, j * PIECE : (j + 1) * PIECE]
        hidden += fc1b_ref[...]
        cdf = 0.5 * (1.0 + lax.erf(hidden * 0.7071067811865476))
        density = jnp.exp(-0.5 * hidden * hidden) * 0.3989422804014327
        slope[...] = cdf + hidden * density
        act[:, 0:PIECE] = (hidden * cdf).astype(BF16)
        spread("mn", lambda k: mns.at[8 * core + k], mnr)
        spread("act", lambda k: act, actr)

    my_slot = dp * 2 + phase

    def target(k):
        return (2 * core + k // 4, (k // 2) % 2 * 2 + k % 2, ten)

    def is_self(k):
        to = target(k)
        return (to[0] == dp) & (to[1] == pipe)

    def spread(name, source, slots):
        for k in range(8):
            number = sems(name, k)

            def send(k=k, number=number):
                pltpu.make_async_remote_copy(
                    src_ref=source(k),
                    dst_ref=slots.at[my_slot],
                    send_sem=send_sem.at[number],
                    recv_sem=recv_sem.at[sems(name, "got") + my_slot],
                    device_id=target(k),
                    device_id_type=MESH,
                ).start()

            def keep(k=k, number=number):
                pltpu.make_async_copy(
                    source(k), slots.at[my_slot], recv_sem.at[sems(name, "got") + my_slot]
                ).start()

            pl.when(jnp.logical_not(is_self(k)))(send)
            pl.when(is_self(k))(keep)

    def spread_numbers():
        for name in ("mn", "act", "gp", "vis"):
            sems(name, "got")
            for i in range(1, 8):
                sems(name, "got+", i)
            for k in range(8):
                sems(name, k)

    spread_numbers()

    def collect(name, slots):
        for i in range(8):
            pltpu.make_async_copy(
                slots.at[i], slots.at[i], recv_sem.at[sems(name, "got") + i]
            ).wait()

    def drain_spread(name, source):
        for k in range(8):
            number = sems(name, k)

            @pl.when(jnp.logical_not(is_self(k)))
            def _(k=k, number=number):
                pltpu.make_async_copy(source(k), source(k), send_sem.at[number]).wait()

    vis_gather = Gather(("vis",), vis, BLK, jnp.where(upper, 1 - zl, zl))

    @pl.when(upper)
    def _():
        out = []
        scatters = {}
        for m in (1, 0):
            tg_gathers[m].last()
            flat = tg[m].reshape(8 * 48, 1024)
            for e in range(4):
                wide = nn(tgsel_ref[e], flat).astype(BF16)
                inc[m, 2 * e] = wide[:, 0:BLK]
                inc[m, 2 * e + 1] = wide[:, BLK : 2 * BLK]
            if m == 1:
                lo.wait()
                arrive(("wo",), wo.at[pl.ds((1 - core) * 256, 256), :])
            out.append(head_grads(m))
            out.extend(backward(m))
            scatters[m] = scatter_first(m, SEQ, acts[m])

        for m in (1, 0):
            for z in range(2):
                scatters[m].second(z)
            scatters[m].third()
        for m in (1, 0):
            total = scatters[m].result()
            inner = to_column(inner_row(m))
            scale = sc[m][:, 0:1]
            cols = pl.ds(pl.multiple_of(ten * BLK, BLK), BLK)
            unit = xb[m, :, cols].astype(F32) * scale
            w = total * gb[ten]
            out_block[m] = (inc[m, ten].astype(F32) + scale * (w - unit * inner)).astype(BF16)
            out.append(remote(("down", m), out_block.at[m], inc.at[m, ten], cross))
        merger_forward()
        for copy in out:
            copy.wait_send()
        for m in (1, 0):
            tg_gathers[m].drain()
            scatters[m].drain()
        arrive(("up",), vis.at[(1 - zl) * 4 + xx])
        vis_gather.start()
        vis_gather.rest()
        vis_gather.drain()

    @pl.when(jnp.logical_not(upper))
    def _():
        merger_forward()
        lo.wait()
        arrive(("wo",), wo.at[pl.ds((1 - core) * 256, 256), :])
        out = []
        gathers = {m: Gather(("inc", m), inc.at[m], BLK, 1 - zl) for m in range(2)}
        scatters = {}
        picks = {}
        for m in (1, 0):
            arrive(("down", m), inc.at[m, (1 - zl) * 4 + xx])
            gathers[m].start()
            gathers[m].rest()
            out.append(head_grads(m))
            out.extend(backward(m))
            wide = lax.broadcasted_iota(jnp.int32, (VIS, SEQ), 0) + m * VIS
            across = lax.broadcasted_iota(jnp.int32, (VIS, SEQ), 1)
            tokens = jnp.sum(
                jnp.where(across == wide, pos_ref[...], 0), axis=1, keepdims=True
            )
            picks[m] = (tokens - m * SEQ) == across
            pick = jnp.where(picks[m], 1.0, 0.0).astype(BF16)
            scatters[m] = scatter_first(m, VIS, nn(pick, acts[m]).astype(BF16))
        for m in (1, 0):
            for z in range(2):
                scatters[m].second(z)
            scatters[m].third()
        for m in (1, 0):
            total = scatters[m].result()
            mask = picks[m]
            pick = jnp.where(mask, 1.0, 0.0).astype(BF16)
            inner = jnp.sum(jnp.where(mask, inner_row(m), 0.0), axis=1, keepdims=True)
            scale_row = to_row(sc[m][:, 0:1])
            scale = jnp.sum(jnp.where(mask, scale_row, 0.0), axis=1, keepdims=True)
            cols = pl.ds(pl.multiple_of(ten * BLK, BLK), BLK)
            unit = nn(pick, xb[m, :, cols]) * scale
            w = total * gb[ten]
            block = (nn(pick, inc[m, ten]) + scale * (w - unit * inner)).astype(BF16)
            if m == 1:
                out_block[0, 0:VIS, :] = block
                out.append(
                    remote(("up",), out_block.at[0, pl.ds(0, VIS), :], vis.at[ten], cross)
                )
            else:
                vis[ten] = block
        vis_gather.start()
        vis_gather.rest()
        for copy in out:
            copy.wait_send()
        for m in (1, 0):
            gathers[m].drain()
            scatters[m].drain()
        vis_gather.drain()

    spread("vis", lambda k: vis.at[k], visr)
    ga_own[...] = jnp.zeros_like(ga_own)
    for i in range(8):
        ga_own[...] += nt(vis[i], f2[:, i * BLK : (i + 1) * BLK])
    sent.append(remote(("ga",), ga_own, ga_other, sibling))
    arrive(("ga",), ga_other)
    grad_pre = ((ga_own[...] + ga_other[...]) * slope[...]).astype(BF16)
    gpre[:, 0:PIECE] = grad_pre
    spread("gp", lambda k: gpre, gpr)
    stat_lane = lax.broadcasted_iota(jnp.int32, (VIS, LANES - PIECE), 1)
    for q in range(2):
        cols = pl.ds(pl.multiple_of(core * 2 * CTX + q * CTX, CTX), CTX)
        gm = nn(grad_pre, f1[:, cols])
        u = gm * lng_ref[...]
        n = jnp.concatenate([pu[0, 2 * core + q], pu[1, 2 * core + q]], axis=0)
        s1 = jnp.sum(u, axis=1, keepdims=True)
        s2 = jnp.sum(u * n, axis=1, keepdims=True)
        h1 = s1.astype(BF16).astype(F32)
        h2 = s2.astype(BF16).astype(F32)
        stats = jnp.where(
            stat_lane == 0,
            h1,
            jnp.where(
                stat_lane == 1,
                s1 - h1,
                jnp.where(stat_lane == 2, h2, jnp.where(stat_lane == 3, s2 - h2, 0.0)),
            ),
        ).astype(BF16)
        for j in range(4):
            pgp[q * 4 + j, :, 0:PIECE] = gm[:, j * PIECE : (j + 1) * PIECE].astype(BF16)
            pgp[q * 4 + j, :, PIECE:LANES] = stats
    for o in range(1, 8):
        to = lax.rem(ten + o, 8)
        sent.append(remote(("pg", o), pgp.at[to], pgpr.at[ten], device(t=to)))

    collect("act", actr)
    collect("vis", visr)
    fc2_out[...] = tn(
        actr[...].reshape(8 * VIS, LANES)[:, 0:PIECE], visr[...].reshape(8 * VIS, BLK)
    )

    total = pgp[ten].astype(F32)
    for o in range(1, 8):
        src = lax.rem(ten + 8 - o, 8)
        arrive(("pg", o), pgpr.at[src])
        total += pgpr[src].astype(F32)
    s1 = (total[:, PIECE : PIECE + 1] + total[:, PIECE + 1 : PIECE + 2]) / CTX
    s2 = (total[:, PIECE + 2 : PIECE + 3] + total[:, PIECE + 3 : PIECE + 4]) / CTX
    patch = 2 * core + zl
    inv = jnp.concatenate([iv[0, patch], iv[1, patch]], axis=0)[:, 0:1]
    block = inv * (total[:, 0:PIECE] * lgb[xx] - s1 - nblk[ten] * s2)
    for b in range(2):
        rows = jnp.concatenate(
            [block[b * 24 : (b + 1) * 24, :], jnp.zeros((8, PIECE), F32)], axis=0
        )
        pgs[b, :, 0:PIECE] = rows.astype(BF16)
    my_code = core * 8 + ten
    for o in range(1, 16):
        code = lax.rem(my_code + o, 16)
        sent.append(
            remote(
                ("po", o),
                pgs.at[code // 8],
                pgr.at[my_code],
                device(b=code // 8, t=lax.rem(code, 8)),
            )
        )
    pgr[my_code] = pgs[core]

    collect("mn", mnr)
    collect("gp", gpr)
    fc1_out[...] = tn(
        mnr[...].reshape(8 * VIS, LANES)[:, 0:PIECE], gpr[...].reshape(8 * VIS, LANES)[:, 0:PIECE]
    )
    for o in range(1, 16):
        arrive(("po", o), pgr.at[lax.rem(my_code + 16 - o, 16)])
    pg_out[...] = pgr[...]

    for copy in sent:
        copy.wait_send()
    drain_spread("mn", lambda k: mns.at[8 * core + k])
    drain_spread("act", lambda k: act)
    drain_spread("gp", lambda k: gpre)
    drain_spread("vis", lambda k: vis.at[k])


def tables():
    freq = THETA ** (-(2.0 * np.arange(64, dtype=np.float64)) / HEAD)
    angles = np.arange(SEQ, dtype=np.float64)[:, None] * freq[None, :]
    cosine, sine = np.cos(angles), np.sin(angles)
    pick = np.zeros((4, SEQ, 8 * 48), np.float32)
    for e in range(4):
        for t in range(8):
            for i in range(12):
                pick[e, t * 12 + i, t * 48 + e * 12 + i] = 1.0
    return (
        np.concatenate([cosine, cosine], axis=1).astype(np.float32),
        np.concatenate([-sine, sine], axis=1).astype(np.float32),
        pick,
    )


def local(
    lm_inputs,
    top_grad,
    phase_gain,
    query_weight,
    kv_weight,
    out_weight,
    segment_ids,
    visual_pos,
    patches,
    ln_gain,
    ln_bias,
    fc1_weight,
    fc1_bias,
    fc2_weight,
):
    cosine, sine, pick = tables()
    shards = top_grad[0].reshape(2, 12, 2, 4, 1024).transpose(0, 2, 3, 1, 4)
    shards = shards.reshape(2, 2, 48, 1024)
    vmem = pl.BlockSpec(memory_space=pltpu.VMEM)
    hbm = pl.BlockSpec(memory_space=pl.ANY)
    v = pltpu.VMEM
    pg, fc1_grad, fc2_grad = pl.pallas_call(
        kernel,
        out_shape=(
            jax.ShapeDtypeStruct((16, 32, LANES), BF16),
            jax.ShapeDtypeStruct((PIECE, PIECE), F32),
            jax.ShapeDtypeStruct((PIECE, BLK), F32),
        ),
        in_specs=[
            hbm, hbm, vmem, hbm, hbm, hbm, vmem, vmem, vmem, vmem, vmem, hbm, vmem, hbm,
            vmem, vmem, vmem,
        ],
        out_specs=(vmem, vmem, vmem),
        scratch_shapes=[
            v((3, HALF, 256), BF16),
            v((512, HALF), BF16),
            v((PIECE, 4 * CTX), BF16),
            v((PIECE, HALF), BF16),
            v((SEQ, WIDTH), BF16),
            v((2, SEQ, HALF), BF16),
            v((2, SEQ, HEAD), F32),
            v((8, 1, BLK), F32),
            v((2, 8, 48, 1024), BF16),
            v((2, 8, SEQ, BLK), BF16),
            v((2 * SEQ, 768), F32),
            v((2 * SEQ, 768), F32),
            v((2 * SEQ, 768), F32),
            v((2, 4 * SEQ, HEAD), BF16),
            v((2, SEQ, HEAD), BF16),
            v((2, SEQ, HEAD), BF16),
            v((2, 4 * SEQ, SEQ), F32),
            v((2, SEQ, 512), F32),
            v((2, SEQ, 512), F32),
            v((2, SEQ, 768), BF16),
            v((2, 8, HEAD), F32),
            v((2, 8, 8, HEAD), F32),
            v((2, 8, SEQ, BLK), BF16),
            v((2, 2, 2, SEQ, 256), BF16),
            v((2, 2, 2, SEQ, BLK), BF16),
            v((2, SEQ, BLK), BF16),
            v((2, SEQ, BLK), BF16),
            v((2, SEQ, BLK), F32),
            v((2, SEQ, BLK), BF16),
            v((8, VIS, BLK), BF16),
            v((2, 4, 24, CTX), F32),
            v((2, 4, 24, HEAD), F32),
            v((VIS, 4 * CTX), BF16),
            v((16, VIS, LANES), BF16),
            v((VIS, LANES), BF16),
            v((VIS, PIECE), F32),
            v((8, VIS, PIECE), F32),
            v((4, 1, PIECE), F32),
            v((VIS, PIECE), F32),
            v((VIS, PIECE), F32),
            v((VIS, LANES), BF16),
            v((8, VIS, LANES), BF16),
            v((8, VIS, LANES), BF16),
            v((8, VIS, LANES), BF16),
            v((8, VIS, BLK), BF16),
            v((8, VIS, LANES), BF16),
            v((8, VIS, LANES), BF16),
            v((2, 32, LANES), BF16),
            v((16, 32, LANES), BF16),
            pltpu.SemaphoreType.DMA((192,)),
            pltpu.SemaphoreType.DMA((192,)),
            pltpu.SemaphoreType.DMA((12,)),
        ],
        compiler_params=pltpu.CompilerParams(
            collective_id=0, has_side_effects=True, vmem_limit_bytes=60 * 1024 * 1024
        ),
    )(
        lm_inputs[0, 0],
        shards,
        phase_gain,
        query_weight.reshape(WIDTH, 256),
        kv_weight.reshape(WIDTH, HEAD),
        out_weight.reshape(256, WIDTH),
        segment_ids[0],
        visual_pos,
        patches[0],
        ln_gain.reshape(1, CTX),
        ln_bias.reshape(1, CTX),
        fc1_weight.T,
        fc1_bias.reshape(1, PIECE),
        fc2_weight,
        cosine,
        sine,
        jnp.asarray(pick, BF16),
    )
    patch_grad = pg[:, 0:24, 0:PIECE].transpose(1, 0, 2).reshape(1, 24, 4 * CTX)
    return (patch_grad, fc1_grad, fc2_grad.T)


def solution(mesh):
    in_specs = (
        P("dp", "pipe", None, None),
        P("dp", None, "tensor", None),
        P(),
        P("pipe", None, "tensor", None),
        P("pipe", None, "tensor", None),
        P("pipe", "tensor", None, None),
        P("dp", None, None),
        P("dp", None),
        P("dp", "pipe", None),
        P(),
        P(),
        P(None, "tensor"),
        P("tensor"),
        P("tensor", None),
    )
    out_specs = (P("dp", "pipe", None), P(("dp", "pipe"), "tensor"), P(("dp", "pipe"), "tensor"))
    return jax.shard_map(local, mesh=mesh, in_specs=in_specs, out_specs=out_specs, check_vma=False)
```

time: 806 us -> 156 us (0.19); the launches traced: 796 us -> 156 us
  waiting for transfers between devices: 416 us -> 0 us
  Pallas kernels: 0 us -> 143 us
  blocking collectives: 104 us -> 0 us
  local copies, waits for them, and re-layouts: 101 us -> 12 us
  matrix products: 61.7 us -> 0 us
  other arithmetic: 49.2 us -> 0 us
  starting transfers between devices: 48 us -> 0 us
  between operations: 16.4 us -> 0.66 us
    reduce_scatter x2 -> x0, waiting for transfers between devices: 167 us -> none  [the longest x1 86.1 us: local(): lax.psum_scatter(fc2_term.astype(jnp.bfloat16), ('dp', 'pipe'), scatter_d...]
    pallas_call x0 -> x1, Pallas kernels: none -> 143 us  [local(): pl.pallas_call(kernel, out_shape=(jax.ShapeDtypeStruct((16, 32, LANES), B...]
    psum x2 -> x0, waiting for transfers between devices: 127 us -> none  [the longest x1 64.4 us: local(): lax.psum(contract_last(grad_pre, fc1_weight).astype(jnp.bfloat16), 'tensor')]
    unnamed x2 -> x0, blocking collectives: 104 us -> none
    all_gather x4 -> x0, waiting for transfers between devices: 90.2 us -> none  [phase_step(): incoming = lax.all_gather(incoming_rows, 'tensor', axis=0, tiled=True)]
    unnamed x209 -> x2, local copies, waits for them, and re-layouts: 68.3 us -> 3.81 us
    dot_general x39 -> x0, matrix products: 61.7 us -> none  [the longest x14 38.3 us: contract_last(): lax.dot_general(left_side, right_side, (((1,), (1,)), ((), ())), preferre...]
    unnamed x8 -> x0, starting transfers between devices: 24.7 us -> none
  transfers between devices with their start and end apart: 30 -> 0, of which waited for: 13 -> 0; matrix products, arithmetic and copies ran while one was open for 19% -> 0% of each run, Pallas kernels for 0% -> 0%
where the time goes in v1:
time: 156 us
  Pallas kernels  143 us (92%)
  local copies, waits for them, and re-layouts  12 us (8%)
    pallas_call x1, Pallas kernels, local(): pl.pallas_call(kernel, out_shape=(jax.ShapeDtypeStruct((16, 32, LANES), B...  143 us
    unnamed x2, local copies, waits for them, and re-layouts  3.81 us

profile of v1, /device:TPU:1, one launch (start us, length us, event | category | flops | bytes accessed | tf_op | source)
XLA Modules:
  0.0 155.7 jit_solution(2408031784584478927)
XLA Ops:
  0.6 1.3 reshape.36.fc1b_ref
  1.9 1.3 reshape.34.lng_ref
  3.2 1.3 reshape.35.lnb_ref
  4.5 1.2 reshape_squeeze.3
  5.7 0.3 copy.21
  6.1 0.8 copy.22.tg_hbm
  6.9 143.0 %shard_map.184 = (bf16[16,32,384]{2,1,0:T(8,128)(2,1)}, f32[320,320]{1,0:T(8,128)}, f32[320,512]{1,0:T(8,128)}) custom-call(bf16[96,8192]{1,0:T(8,128)(2,1)} %bitcast.19, bf16[2,2,48,1024]{3,2,1,0:T(8,128)(2,1)} %copy.22.tg_hbm, f32[2,8192]{1,0:T(2,128)} %gain_ref.1, bf16[8192,256]{1,0:T(8,128)(2,1)} %bitcast.15, bf16[8192,128]{1,0:T(8,128)(2,1)} %bitcast.18, ...), custom_call_target="tpu_custom_call" | custom-call | tf_op jit(solution)/shard_map/pallas_call | solution.py:851
  149.9 1.0 slice_bitcast_fusion
  150.9 0.9 reshape.37
  151.9 1.8 %copy.26 = f32[320,320]{1,0:T(8,128)} copy(f32[320,320]{1,0:T(8,128)} %get-tuple-element.13) | data formatting | bytes 819200
  153.7 2.0 %copy.27 = f32[512,320]{0,1:T(8,128)} copy(f32[512,320]{0,1:T(8,128)} %bitcast.21) | data formatting | bytes 1310720
  (1 shorter events, 0.0 us)

commit v2 on v1

--- a/solution.py
+++ b/solution.py
@@ -85,12 +85,17 @@
     fc1_hbm,
     fc1b_ref,
     fc2_hbm,
+    cos_hbm,
+    sin_hbm,
+    tgsel_hbm,
+    pg_out,
+    fc1_out,
+    fc2_out,
     cos_ref,
     sin_ref,
     tgsel_ref,
-    pg_out,
-    fc1_out,
-    fc2_out,
+    fc1_val,
+    fc2_val,
     w3,
     wo,
     f1,
@@ -115,10 +120,6 @@
     inr,
     part,
     r1,
-    r2,
-    r3_send,
-    r3,
-    xsum,
     out_block,
     vis,
     pu,
@@ -143,6 +144,7 @@
     send_sem,
     recv_sem,
     local_sem,
+    y_sem,
 ):
     dp = lax.axis_index("dp")
     pipe = lax.axis_index("pipe")
@@ -162,28 +164,16 @@
         return (dp if d is None else d, 2 * s + b, t)
 
     sibling = device(b=1 - core)
-    right_x = lax.rem(xx + 1, 4)
-    left_x = lax.rem(xx + 3, 4)
-    far_x = lax.rem(xx + 2, 4)
-    right = device(x=right_x)
-    left = device(x=left_x)
-    zmate = device(z=1 - zl)
     cross = device(s=1 - phase, z=1 - zl)
 
     barrier = pltpu.get_barrier_semaphore()
-    count = 0
-    for o in range(1, 16):
-        code = lax.rem(core * 8 + ten + o, 16)
-        pl.semaphore_signal(
-            barrier, inc=1, device_id=device(b=code // 8, t=lax.rem(code, 8)), device_id_type=MESH
-        )
-        code = lax.rem(dp * 4 + pipe + o, 16)
-        pl.semaphore_signal(
-            barrier, inc=1, device_id=(code // 4, lax.rem(code, 4), ten), device_id_type=MESH
-        )
-        count += 2
-    pl.semaphore_signal(barrier, inc=1, device_id=cross, device_id_type=MESH)
-    count += 1
+    up_y = device(d=lax.rem(dp + 1, 4))
+    down_y = device(d=lax.rem(dp + 3, 4))
+    greeted = [sibling, up_y, down_y, device(s=1 - phase)]
+    greeted += [device(t=lax.rem(ten + o, 8)) for o in range(1, 8)]
+    greeted += [device(s=1 - phase, z=1 - zl, x=lax.rem(xx + o, 4)) for o in range(4)]
+    for to in greeted:
+        pl.semaphore_signal(barrier, inc=1, device_id=to, device_id_type=MESH)
 
     def local(name, src, dst):
         copy = pltpu.make_async_copy(src, dst, local_sem.at[locals_(name)])
@@ -215,153 +205,117 @@
         "kv", wkv_hbm.at[pl.ds(mine, HALF), :], w3.at[2, :, pl.ds(core * HEAD, HEAD)]
     )
     lo = local("o", wo_hbm.at[:, pl.ds(mine, HALF)], wo.at[pl.ds(core * 256, 256), :])
+    lsel = local("sel", tgsel_hbm, tgsel_ref)
+    lcos = local("cos", cos_hbm, cos_ref)
+    lsin = local("sin", sin_hbm, sin_ref)
     lf1 = local("f1", fc1_hbm, f1)
     lf2 = local("f2", fc2_hbm.at[:, pl.ds(mine, HALF)], f2)
 
-    pl.semaphore_wait(barrier, count)
-
-    class Gather:
-        def __init__(self, name, ref, width, hz):
-            self.name, self.ref, self.width = name, ref, width
-            self.slots = {
-                "h": hz * 4 + xx,
-                "hr": hz * 4 + right_x,
-                "hl": hz * 4 + left_x,
-                "hf": hz * 4 + far_x,
-                "k": (1 - hz) * 4 + xx,
-                "kr": (1 - hz) * 4 + right_x,
-                "kl": (1 - hz) * 4 + left_x,
-                "kf": (1 - hz) * 4 + far_x,
-            }
-            self.sent = []
-
-        def view(self, slot, part_):
-            ref = self.ref.at[self.slots[slot]]
-            if part_ is not None:
-                ref = ref.at[:, pl.ds(part_ * (self.width // 2), self.width // 2)]
-            return ref
-
-        def send(self, tag, slot, to, part_=None):
-            ref = self.view(slot, part_)
-            self.sent.append((sems(self.name, tag), ref))
-            remote((self.name, tag), ref, ref, to)
-
-        def got(self, tag, slot, part_=None):
-            arrive((self.name, tag), self.view(slot, part_))
-
-        def start(self):
-            self.sent = []
-            self.send("r1", "h", right)
-            self.send("l1", "h", left)
-            self.send("z", "h", zmate)
-
-        def second(self):
-            self.got("z", "k")
-            self.send("r2", "k", right)
-            self.send("l2", "k", left)
-
-        def third(self):
-            self.got("r1", "hl")
-            self.send("fr1", "hl", right, 0)
-            self.got("l1", "hr")
-            self.send("fl1", "hr", left, 1)
-
-        def fourth(self):
-            self.got("r2", "kl")
-            self.send("fr2", "kl", right, 0)
-            self.got("l2", "kr")
-            self.send("fl2", "kr", left, 1)
-
-        def last(self):
-            self.got("fr1", "hf", 0)
-            self.got("fl1", "hf", 1)
-            self.got("fr2", "kf", 0)
-            self.got("fl2", "kf", 1)
-
-        def rest(self):
-            self.second()
-            self.third()
-            self.fourth()
-            self.last()
-
-        def drain(self):
-            for number, ref in self.sent:
-                pltpu.make_async_copy(ref, ref, send_sem.at[number]).wait()
-
-    class Scatter:
-        def __init__(self, m, rows):
-            self.m, self.rows, self.sent = m, rows, []
-
-        def block(self, z, x, cols=None):
-            cols = slice(None) if cols is None else pl.ds(cols * 256, 256)
-            return part.at[self.m, z * 4 + x, pl.ds(0, self.rows), cols]
-
-        def one(self, side, z):
-            return r1.at[self.m, side, z, pl.ds(0, self.rows), :]
-
-        def two(self, side, z):
-            return r2.at[self.m, side, z, pl.ds(0, self.rows), :]
-
-        def three(self, ref):
-            return ref.at[self.m, pl.ds(0, self.rows), :]
-
-        def first(self, z):
-            self.sent.append(
-                remote(("s1r", self.m, z), self.block(z, far_x, 0), self.one(0, z), right)
-            )
-            self.sent.append(
-                remote(("s1l", self.m, z), self.block(z, far_x, 1), self.one(1, z), left)
-            )
-
-        def second(self, z):
-            arrive(("s1r", self.m, z), self.one(0, z))
-            ref = self.block(z, right_x, 0)
-            ref[...] = (ref[...].astype(F32) + self.one(0, z)[...].astype(F32)).astype(BF16)
-            self.sent.append(
-                remote(("s2r", self.m, z), self.block(z, right_x), self.two(0, z), right)
-            )
-            arrive(("s1l", self.m, z), self.one(1, z))
-            ref = self.block(z, left_x, 1)
-            ref[...] = (ref[...].astype(F32) + self.one(1, z)[...].astype(F32)).astype(BF16)
-            self.sent.append(
-                remote(("s2l", self.m, z), self.block(z, left_x), self.two(1, z), left)
-            )
-
-        def total(self, z):
-            return (
-                self.block(z, xx)[...].astype(F32)
-                + self.two(0, z)[...].astype(F32)
-                + self.two(1, z)[...].astype(F32)
-            )
-
-        def third(self):
-            for z in range(2):
-                arrive(("s2r", self.m, z), self.two(0, z))
-                arrive(("s2l", self.m, z), self.two(1, z))
-            self.three(r3_send)[...] = self.total(1 - zl).astype(BF16)
-            self.sent.append(
-                remote(("s3", self.m), self.three(r3_send), self.three(r3), zmate)
-            )
-            self.three(xsum)[...] = self.total(zl)
-
-        def result(self):
-            arrive(("s3", self.m), self.three(r3))
-            return self.three(xsum)[...] + self.three(r3)[...].astype(F32)
-
-        def drain(self):
-            for copy in self.sent:
-                copy.wait_send()
+    pl.semaphore_wait(barrier, len(greeted))
+
+    def peer(o):
+        return lax.rem(ten + o, 8)
+
+    def push(name, src, slots, slot, to=None):
+        return [remote((name, o), src, slots.at[slot], device(t=peer(o))) for o in range(1, 8)]
+
+    def terms(m):
+        return r1.at[m]
+
+    def send_terms(m, rows, left_side):
+        out = []
+        for o in list(range(1, 8)) + [0]:
+            j = peer(o)
+            cols = pl.ds(pl.multiple_of(j * BLK, BLK), BLK)
+            acc = nt(left_side[:, 0:256], w3[0, cols, :])
+            acc += nt(left_side[:, 256:512], w3[1, cols, :])
+            acc += nt(left_side[:, 512:768], w3[2, cols, :])
+            part[m, j, pl.ds(0, rows), :] = acc.astype(BF16)
+            if o:
+                out.append(
+                    remote(
+                        ("rs", m, o),
+                        part.at[m, j, pl.ds(0, rows), :],
+                        r1.at[m, ten, pl.ds(0, rows), :],
+                        device(t=j),
+                    )
+                )
+        return out
+
+    def sum_terms(m, rows):
+        total = part[m, ten, pl.ds(0, rows), :].astype(F32)
+        for o in range(1, 8):
+            src = peer(8 - o)
+            ref = r1.at[m, src, pl.ds(0, rows), :]
+            arrive(("rs", m, o), ref)
+            total += ref[...].astype(F32)
+        return total
 
     sent = []
-    tg_gathers = {m: Gather(("tg", m), tg.at[m], 1024, zl) for m in range(2)}
     upper = phase == 1
-
-    @pl.when(upper)
-    def _():
+    lower = jnp.logical_not(upper)
+    cut_at = 384
+
+    for m in (1, 0):
+
+        @pl.when(upper)
+        def _(m=m):
+            local(("tg", m), tg_hbm.at[m, core], tg.at[m, ten])
+            for o in range(1, 4):
+                remote(
+                    ("tgx", m, o),
+                    tg_hbm.at[m, core],
+                    tg.at[m, ten],
+                    device(x=lax.rem(xx + o, 4)),
+                )
+            for o in range(4):
+                remote(
+                    ("tgz", m, o),
+                    tg_hbm.at[m, core, :, pl.ds(0, cut_at)],
+                    tg.at[m, ten, :, pl.ds(0, cut_at)],
+                    device(z=1 - zl, x=lax.rem(xx + o, 4)),
+                )
+
+        @pl.when(lower)
+        def _(m=m):
+            for o in range(4):
+                remote(
+                    ("tgc", m, o),
+                    tg_hbm.at[m, core, :, pl.ds(cut_at, 1024 - cut_at)],
+                    tg.at[m, ten, :, pl.ds(cut_at, 1024 - cut_at)],
+                    device(s=1, z=1 - zl, x=lax.rem(xx + o, 4)),
+                )
+
+    def tg_wait(m):
+        pltpu.make_async_copy(
+            tg.at[m, ten], tg.at[m, ten], local_sem.at[locals_(("tg", m))]
+        ).wait()
+        for o in range(1, 4):
+            arrive(("tgx", m, o), tg.at[m, zl * 4 + lax.rem(xx + 4 - o, 4)])
+        for o in range(4):
+            slot = (1 - zl) * 4 + lax.rem(xx + 4 - o, 4)
+            arrive(("tgz", m, o), tg.at[m, slot, :, pl.ds(0, cut_at)])
+            arrive(("tgc", m, o), tg.at[m, slot, :, pl.ds(cut_at, 1024 - cut_at)])
+
+    def sent_wait(name, ref):
+        pltpu.make_async_copy(ref, ref, send_sem.at[sems(*name)]).wait()
+
+    def tg_drain():
         for m in (1, 0):
-            copy = local(("tg", m), tg_hbm.at[m, core], tg.at[m, ten])
-            copy.wait()
-            tg_gathers[m].start()
+
+            @pl.when(upper)
+            def _(m=m):
+                for o in range(1, 4):
+                    sent_wait(("tgx", m, o), tg_hbm.at[m, core])
+                for o in range(4):
+                    sent_wait(("tgz", m, o), tg_hbm.at[m, core, :, pl.ds(0, cut_at)])
+
+            @pl.when(lower)
+            def _(m=m):
+                for o in range(4):
+                    sent_wait(
+                        ("tgc", m, o), tg_hbm.at[m, core, :, pl.ds(cut_at, 1024 - cut_at)]
+                    )
 
     sent.append(remote(("x",), x_hbm.at[:, pl.ds(theirs, HALF)], xb.at[core], sibling))
     sent.append(remote(("wq",), wq_hbm.at[pl.ds(theirs, HALF), :], w3.at[core], sibling))
@@ -397,21 +351,6 @@
     sc[core] = jnp.broadcast_to(lax.rsqrt(acc / WIDTH + EPS_RMS), (SEQ, HEAD))
     sent.append(remote(("sc",), sc.at[core], sc.at[core], sibling))
 
-    for q in range(4):
-        v = patches_ref[:, q * CTX : (q + 1) * CTX].astype(F32)
-        v = v - jnp.mean(v, axis=1, keepdims=True)
-        inv = lax.rsqrt(jnp.mean(v * v, axis=1, keepdims=True) + EPS_LN)
-        pu[core, q] = v * inv
-        iv[core, q] = jnp.broadcast_to(inv, (24, HEAD))
-    sent.append(remote(("pu",), pu.at[core], pu.at[core], sibling))
-    sent.append(remote(("iv",), iv.at[core], iv.at[core], sibling))
-
-    @pl.when(upper)
-    def _():
-        for m in (1, 0):
-            tg_gathers[m].second()
-            tg_gathers[m].third()
-
     lxh.wait()
     lq.wait()
     lkv.wait()
@@ -432,11 +371,6 @@
 
     each(8, project)
     sent.append(remote(("p",), own_p, other_p, sibling))
-
-    @pl.when(upper)
-    def _():
-        for m in (1, 0):
-            tg_gathers[m].fourth()
 
     arrive(("p",), other_p)
     pf[...] = own_p[...] + other_p[...]
@@ -463,7 +397,7 @@
         ks[m] = k
         vs[m] = v
         scores = nt(q, k) * FACTOR
-        seg = seg_ref[m : m + 1, :].astype(F32)
+        seg = seg_ref[0, m : m + 1, :].astype(F32)
         seg_col = to_column(seg)
         index_row = lax.broadcasted_iota(jnp.int32, (SEQ, SEQ), 0)
         index_col = lax.broadcasted_iota(jnp.int32, (SEQ, SEQ), 1)
@@ -474,17 +408,17 @@
         weights = jnp.where(allowed, jnp.exp(scores - top), 0.0)
         probs[m] = weights / jnp.sum(weights, axis=1, keepdims=True)
 
+    lcos.wait()
+    lsin.wait()
     for m in (1, 0):
         forward(m)
 
-    def head_grads(m):
-        gx_own[m] = jnp.zeros((SEQ, 512), F32)
-
-        def step(i):
-            cols = pl.ds(pl.multiple_of(i * BLK, BLK), BLK)
-            gx_own[m] += nt(inc[m, i], wo[:, cols])
-
-        each(8, step)
+    def head_grads(m, slots):
+        acc = jnp.zeros((SEQ, 512), F32)
+        for slot in slots():
+            cols = pl.ds(pl.multiple_of(slot * BLK, BLK), BLK)
+            acc += nt(inc[m, slot], wo[:, cols])
+        gx_own[m] = acc
         return remote(("gx", m), gx_own.at[m], gx_other.at[m], sibling)
 
     def backward(m):
@@ -513,43 +447,37 @@
         ins[m, :, 0:SEQ] = jnp.broadcast_to(row, (8, SEQ))
         out = []
         for o in range(1, 8):
-            to = lax.rem(ten + o, 8)
-            out.append(remote(("in", m, o), ins.at[m], inr.at[m, ten], device(t=to)))
+            out.append(remote(("in", m, o), ins.at[m], inr.at[m, ten], device(t=peer(o))))
         return out
 
     def inner_row(m):
         total = ins[m, 0:1, 0:SEQ]
         for o in range(1, 8):
-            src = lax.rem(ten + 8 - o, 8)
+            src = peer(8 - o)
             arrive(("in", m, o), inr.at[m, src])
             total += inr[m, src, 0:1, 0:SEQ]
         return total
 
-    def back_project(m, z, x, left_side):
-        i = z * 4 + x
-        rows = pl.ds(pl.multiple_of(i * BLK, BLK), BLK)
-        acc = nt(left_side[:, 0:256], w3[0, rows, :])
-        acc += nt(left_side[:, 256:512], w3[1, rows, :])
-        acc += nt(left_side[:, 512:768], w3[2, rows, :])
-        part[m, i, pl.ds(0, left_side.shape[0]), :] = acc.astype(BF16)
-
-    def scatter_first(m, rows, left_side):
-        s = Scatter(m, rows)
-        for z in range(2):
-            back_project(m, z, far_x, left_side)
-            s.first(z)
-        for x in (right_x, left_x, xx):
-            for z in range(2):
-                back_project(m, z, x, left_side)
-        return s
-
     def merger_forward():
+        for q in range(4):
+            v = patches_ref[0, :, q * CTX : (q + 1) * CTX].astype(F32)
+            v = v - jnp.mean(v, axis=1, keepdims=True)
+            inv = lax.rsqrt(jnp.mean(v * v, axis=1, keepdims=True) + EPS_LN)
+            pu[core, q] = v * inv
+            iv[core, q] = jnp.broadcast_to(inv, (24, HEAD))
+        remote(("pu",), pu.at[core], pu.at[core], sibling)
+        remote(("iv",), iv.at[core], iv.at[core], sibling)
+        for name in ("y1", "y2"):
+            number = ("y1", "y2").index(name)
+            for to in (up_y, down_y):
+                pl.semaphore_signal(y_sem.at[number], inc=1, device_id=to, device_id_type=MESH)
+            pl.semaphore_wait(y_sem.at[number], 2)
         lf1.wait()
         lf2.wait()
         arrive(("pu",), pu.at[1 - core])
         arrive(("iv",), iv.at[1 - core])
-        gain = lng_ref[...]
-        bias = lnb_ref[...]
+        gain = lng_ref[...].reshape(1, CTX)
+        bias = lnb_ref[...].reshape(1, CTX)
         hidden = jnp.zeros((VIS, PIECE), F32)
         for q in range(4):
             n = jnp.concatenate([pu[0, q], pu[1, q]], axis=0)
@@ -563,7 +491,7 @@
             n = jnp.concatenate([pu[0, 2 * core + q], pu[1, 2 * core + q]], axis=0)
             for j in range(4):
                 nblk[q * 4 + j] = n[:, j * PIECE : (j + 1) * PIECE]
-        hidden += fc1b_ref[...]
+        hidden += fc1b_ref[...].reshape(1, PIECE)
         cdf = 0.5 * (1.0 + lax.erf(hidden * 0.7071067811865476))
         density = jnp.exp(-0.5 * hidden * hidden) * 0.3989422804014327
         slope[...] = cdf + hidden * density
@@ -626,32 +554,26 @@
             def _(k=k, number=number):
                 pltpu.make_async_copy(source(k), source(k), send_sem.at[number]).wait()
 
-    vis_gather = Gather(("vis",), vis, BLK, jnp.where(upper, 1 - zl, zl))
-
     @pl.when(upper)
     def _():
         out = []
-        scatters = {}
         for m in (1, 0):
-            tg_gathers[m].last()
+            tg_wait(m)
+            if m == 1:
+                lsel.wait()
+                lo.wait()
+                arrive(("wo",), wo.at[pl.ds((1 - core) * 256, 256), :])
             flat = tg[m].reshape(8 * 48, 1024)
             for e in range(4):
                 wide = nn(tgsel_ref[e], flat).astype(BF16)
                 inc[m, 2 * e] = wide[:, 0:BLK]
                 inc[m, 2 * e + 1] = wide[:, BLK : 2 * BLK]
-            if m == 1:
-                lo.wait()
-                arrive(("wo",), wo.at[pl.ds((1 - core) * 256, 256), :])
-            out.append(head_grads(m))
+            out.append(head_grads(m, lambda: range(8)))
+        for m in (1, 0):
             out.extend(backward(m))
-            scatters[m] = scatter_first(m, SEQ, acts[m])
-
+            out.extend(send_terms(m, SEQ, acts[m]))
         for m in (1, 0):
-            for z in range(2):
-                scatters[m].second(z)
-            scatters[m].third()
-        for m in (1, 0):
-            total = scatters[m].result()
+            total = sum_terms(m, SEQ)
             inner = to_column(inner_row(m))
             scale = sc[m][:, 0:1]
             cols = pl.ds(pl.multiple_of(ten * BLK, BLK), BLK)
@@ -662,43 +584,45 @@
         merger_forward()
         for copy in out:
             copy.wait_send()
-        for m in (1, 0):
-            tg_gathers[m].drain()
-            scatters[m].drain()
-        arrive(("up",), vis.at[(1 - zl) * 4 + xx])
-        vis_gather.start()
-        vis_gather.rest()
-        vis_gather.drain()
-
-    @pl.when(jnp.logical_not(upper))
+        for o in range(8):
+            arrive(("up", o), vis.at[peer(8 - o)])
+
+    @pl.when(lower)
     def _():
         merger_forward()
+        lsel.wait()
         lo.wait()
         arrive(("wo",), wo.at[pl.ds((1 - core) * 256, 256), :])
         out = []
-        gathers = {m: Gather(("inc", m), inc.at[m], BLK, 1 - zl) for m in range(2)}
-        scatters = {}
+        held = (1 - zl) * 4 + xx
+
+        def pass_on(m):
+            arrive(("down", m), inc.at[m, held])
+            out.extend(push(("inc", m), inc.at[m, held], inc.at[m], held))
+
+        def blocks(m):
+            yield held
+            for o in range(1, 8):
+                if m == 1 and o == 5:
+                    pass_on(0)
+                src = peer(8 - o)
+                slot = lax.rem(src + 4, 8)
+                arrive((("inc", m), o), inc.at[m, slot])
+                yield slot
+
+        pass_on(1)
         picks = {}
         for m in (1, 0):
-            arrive(("down", m), inc.at[m, (1 - zl) * 4 + xx])
-            gathers[m].start()
-            gathers[m].rest()
-            out.append(head_grads(m))
+            out.append(head_grads(m, lambda: blocks(m)))
             out.extend(backward(m))
             wide = lax.broadcasted_iota(jnp.int32, (VIS, SEQ), 0) + m * VIS
             across = lax.broadcasted_iota(jnp.int32, (VIS, SEQ), 1)
-            tokens = jnp.sum(
-                jnp.where(across == wide, pos_ref[...], 0), axis=1, keepdims=True
-            )
+            tokens = jnp.sum(jnp.where(across == wide, pos_ref[...], 0), axis=1, keepdims=True)
             picks[m] = (tokens - m * SEQ) == across
             pick = jnp.where(picks[m], 1.0, 0.0).astype(BF16)
-            scatters[m] = scatter_first(m, VIS, nn(pick, acts[m]).astype(BF16))
+            out.extend(send_terms(m, VIS, nn(pick, acts[m]).astype(BF16)))
         for m in (1, 0):
-            for z in range(2):
-                scatters[m].second(z)
-            scatters[m].third()
-        for m in (1, 0):
-            total = scatters[m].result()
+            total = sum_terms(m, VIS)
             mask = picks[m]
             pick = jnp.where(mask, 1.0, 0.0).astype(BF16)
             inner = jnp.sum(jnp.where(mask, inner_row(m), 0.0), axis=1, keepdims=True)
@@ -710,19 +634,22 @@
             block = (nn(pick, inc[m, ten]) + scale * (w - unit * inner)).astype(BF16)
             if m == 1:
                 out_block[0, 0:VIS, :] = block
-                out.append(
-                    remote(("up",), out_block.at[0, pl.ds(0, VIS), :], vis.at[ten], cross)
-                )
+                for o in range(8):
+                    out.append(
+                        remote(
+                            ("up", o),
+                            out_block.at[0, pl.ds(0, VIS), :],
+                            vis.at[ten],
+                            device(s=1, t=peer(o)),
+                        )
+                    )
             else:
                 vis[ten] = block
-        vis_gather.start()
-        vis_gather.rest()
+                out.extend(push("visp", vis.at[ten], vis, ten))
+        for o in range(1, 8):
+            arrive(("visp", o), vis.at[peer(8 - o)])
         for copy in out:
             copy.wait_send()
-        for m in (1, 0):
-            gathers[m].drain()
-            scatters[m].drain()
-        vis_gather.drain()
 
     spread("vis", lambda k: vis.at[k], visr)
     ga_own[...] = jnp.zeros_like(ga_own)
@@ -737,7 +664,7 @@
     for q in range(2):
         cols = pl.ds(pl.multiple_of(core * 2 * CTX + q * CTX, CTX), CTX)
         gm = nn(grad_pre, f1[:, cols])
-        u = gm * lng_ref[...]
+        u = gm * lng_ref[...].reshape(1, CTX)
         n = jnp.concatenate([pu[0, 2 * core + q], pu[1, 2 * core + q]], axis=0)
         s1 = jnp.sum(u, axis=1, keepdims=True)
         s2 = jnp.sum(u * n, axis=1, keepdims=True)
@@ -761,9 +688,10 @@
 
     collect("act", actr)
     collect("vis", visr)
-    fc2_out[...] = tn(
+    fc2_val[...] = tn(
         actr[...].reshape(8 * VIS, LANES)[:, 0:PIECE], visr[...].reshape(8 * VIS, BLK)
     )
+    out2 = local("fc2", fc2_val, fc2_out)
 
     total = pgp[ten].astype(F32)
     for o in range(1, 8):
@@ -776,10 +704,11 @@
     inv = jnp.concatenate([iv[0, patch], iv[1, patch]], axis=0)[:, 0:1]
     block = inv * (total[:, 0:PIECE] * lgb[xx] - s1 - nblk[ten] * s2)
     for b in range(2):
-        rows = jnp.concatenate(
-            [block[b * 24 : (b + 1) * 24, :], jnp.zeros((8, PIECE), F32)], axis=0
-        )
-        pgs[b, :, 0:PIECE] = rows.astype(BF16)
+        rows = block[b * 24 : (b + 1) * 24, :]
+        pgs[b, :, 0:PIECE] = rows[0:16, :].astype(BF16)
+        pgs[b, :, PIECE : PIECE + 160] = jnp.concatenate(
+            [rows[16:24, 0:160], rows[16:24, 160:320]], axis=0
+        ).astype(BF16)
     my_code = core * 8 + ten
     for o in range(1, 16):
         code = lax.rem(my_code + o, 16)
@@ -795,19 +724,39 @@
 
     collect("mn", mnr)
     collect("gp", gpr)
-    fc1_out[...] = tn(
+    fc1_val[...] = tn(
         mnr[...].reshape(8 * VIS, LANES)[:, 0:PIECE], gpr[...].reshape(8 * VIS, LANES)[:, 0:PIECE]
     )
+    out1 = local("fc1", fc1_val, fc1_out)
     for o in range(1, 16):
         arrive(("po", o), pgr.at[lax.rem(my_code + 16 - o, 16)])
-    pg_out[...] = pgr[...]
+    for q in range(4):
+        pieces = []
+        for j in range(4):
+            msg = pgr[q * 4 + j].astype(F32)
+            tail = jnp.concatenate(
+                [msg[0:8, PIECE : PIECE + 160], msg[8:16, PIECE : PIECE + 160]], axis=1
+            )
+            pieces.append(jnp.concatenate([msg[:, 0:PIECE], tail], axis=0))
+        pg_out[0, :, q * CTX : (q + 1) * CTX] = jnp.concatenate(pieces, axis=1).astype(BF16)
 
     for copy in sent:
         copy.wait_send()
+    out1.wait()
+    out2.wait()
+    tg_drain()
+    sent_wait(("pu",), pu.at[core])
+    sent_wait(("iv",), iv.at[core])
     drain_spread("mn", lambda k: mns.at[8 * core + k])
     drain_spread("act", lambda k: act)
     drain_spread("gp", lambda k: gpre)
     drain_spread("vis", lambda k: vis.at[k])
+
+
+def hand_over(a, b, c, a_out, b_out, c_out):
+    a_out[...] = a[...]
+    b_out[...] = b[...]
+    c_out[...] = c[...]
 
 
 def tables():
@@ -851,16 +800,21 @@
     pg, fc1_grad, fc2_grad = pl.pallas_call(
         kernel,
         out_shape=(
-            jax.ShapeDtypeStruct((16, 32, LANES), BF16),
+            jax.ShapeDtypeStruct((1, 24, 4 * CTX), BF16),
             jax.ShapeDtypeStruct((PIECE, PIECE), F32),
             jax.ShapeDtypeStruct((PIECE, BLK), F32),
         ),
         in_specs=[
             hbm, hbm, vmem, hbm, hbm, hbm, vmem, vmem, vmem, vmem, vmem, hbm, vmem, hbm,
-            vmem, vmem, vmem,
+            hbm, hbm, hbm,
         ],
-        out_specs=(vmem, vmem, vmem),
+        out_specs=(vmem, hbm, hbm),
         scratch_shapes=[
+            v((SEQ, HEAD), F32),
+            v((SEQ, HEAD), F32),
+            v((4, SEQ, 8 * 48), BF16),
+            v((PIECE, PIECE), F32),
+            v((PIECE, BLK), F32),
             v((3, HALF, 256), BF16),
             v((512, HALF), BF16),
             v((PIECE, 4 * CTX), BF16),
@@ -884,11 +838,7 @@
             v((2, 8, HEAD), F32),
             v((2, 8, 8, HEAD), F32),
             v((2, 8, SEQ, BLK), BF16),
-            v((2, 2, 2, SEQ, 256), BF16),
-            v((2, 2, 2, SEQ, BLK), BF16),
-            v((2, SEQ, BLK), BF16),
-            v((2, SEQ, BLK), BF16),
-            v((2, SEQ, BLK), F32),
+            v((2, 8, SEQ, BLK), BF16),
             v((2, SEQ, BLK), BF16),
             v((8, VIS, BLK), BF16),
             v((2, 4, 24, CTX), F32),
@@ -908,11 +858,12 @@
             v((8, VIS, BLK), BF16),
             v((8, VIS, LANES), BF16),
             v((8, VIS, LANES), BF16),
-            v((2, 32, LANES), BF16),
-            v((16, 32, LANES), BF16),
-            pltpu.SemaphoreType.DMA((192,)),
-            pltpu.SemaphoreType.DMA((192,)),
-            pltpu.SemaphoreType.DMA((12,)),
+            v((2, 16, BLK), BF16),
+            v((16, 16, BLK), BF16),
+            pltpu.SemaphoreType.DMA((224,)),
+            pltpu.SemaphoreType.DMA((224,)),
+            pltpu.SemaphoreType.DMA((20,)),
+            pltpu.SemaphoreType.REGULAR((2,)),
         ],
         compiler_params=pltpu.CompilerParams(
             collective_id=0, has_side_effects=True, vmem_limit_bytes=60 * 1024 * 1024
@@ -924,20 +875,25 @@
         query_weight.reshape(WIDTH, 256),
         kv_weight.reshape(WIDTH, HEAD),
         out_weight.reshape(256, WIDTH),
-        segment_ids[0],
+        segment_ids,
         visual_pos,
-        patches[0],
-        ln_gain.reshape(1, CTX),
-        ln_bias.reshape(1, CTX),
+        patches,
+        ln_gain,
+        ln_bias,
         fc1_weight.T,
-        fc1_bias.reshape(1, PIECE),
+        fc1_bias,
         fc2_weight,
         cosine,
         sine,
         jnp.asarray(pick, BF16),
     )
-    patch_grad = pg[:, 0:24, 0:PIECE].transpose(1, 0, 2).reshape(1, 24, 4 * CTX)
-    return (patch_grad, fc1_grad, fc2_grad.T)
+    pg, fc1_grad, fc2_grad = pl.pallas_call(
+        hand_over,
+        out_shape=tuple(jax.ShapeDtypeStruct(a.shape, a.dtype) for a in (pg, fc1_grad, fc2_grad)),
+        in_specs=[vmem, vmem, vmem],
+        out_specs=(vmem, vmem, vmem),
+    )(pg, fc1_grad, fc2_grad)
+    return (pg, fc1_grad, fc2_grad.T)
 
 
 def solution(mesh):

time: 156 us -> 115 us (0.74)
  Pallas kernels: 143 us -> 112 us
  local copies, waits for them, and re-layouts: 12 us -> 2.38 us
    pallas_call x1 -> x2, Pallas kernels: 143 us -> 112 us  [the longest x1 110 us: local(): pl.pallas_call(kernel, out_shape=(jax.ShapeDtypeStruct((1, 24, 4 * CTX),...]
    reshape x4 -> x0, local copies, waits for them, and re-layouts: 4.8 us -> none  [the longest x1 1.29 us: local(): ln_gain.reshape(1, CTX)]
    unnamed x2 -> x0, local copies, waits for them, and re-layouts: 3.81 us -> none
where the time goes in v2:
time: 115 us
  Pallas kernels  112 us (97%)
  local copies, waits for them, and re-layouts  2.38 us (2%)
    pallas_call x1, Pallas kernels, local(): pl.pallas_call(kernel, out_shape=(jax.ShapeDtypeStruct((1, 24, 4 * CTX),...  110 us
    pallas_call x1, Pallas kernels, local(): pl.pallas_call(hand_over, out_shape=tuple((jax.ShapeDtypeStruct(a.shape,...  2.47 us

profile of v2, /device:TPU:1, one launch (start us, length us, event | category | flops | bytes accessed | tf_op | source)
XLA Modules:
  0.0 115.3 jit_solution(16804493512622463481)
XLA Ops:
  0.6 1.2 %reshape_squeeze.3 = bf16[2,12,2,4,1024]{4,3,2,0,1:T(4,128)(2,1)S(1)} reshape(bf16[1,2,12,8192]{3,1,2,0:T(2,128)(2,1)} %param.18) | data formatting | bytes 786432 | tf_op jit(solution)/shard_map/reshape;squeeze | solution.py:795
  1.9 0.3 copy.21
  2.2 0.8 copy.22.tg_hbm
  3.0 109.8 %shard_map.184 = (bf16[1,24,5120]{2,1,0:T(8,128)(2,1)}, f32[320,320]{1,0:T(8,128)}, f32[320,512]{1,0:T(8,128)}) custom-call(bf16[96,8192]{1,0:T(8,128)(2,1)} %bitcast.15, bf16[2,2,48,1024]{3,2,1,0:T(8,128)(2,1)} %copy.22.tg_hbm, f32[2,8192]{1,0:T(2,128)} %gain_ref.1, bf16[8192,256]{1,0:T(8,128)(2,1)} %bitcast.11, bf16[8192,128]{1,0:T(8,128)(2,1)} %bitcast.14, ...), custom_call_target="tpu_custom_call" | custom-call | tf_op jit(solution)/shard_map/pallas_call | solution.py:800
  112.8 2.5 %shard_map.185 = (bf16[1,24,5120]{2,1,0:T(8,128)(2,1)}, f32[320,320]{1,0:T(8,128)}, f32[320,512]{1,0:T(8,128)}) custom-call(bf16[1,24,5120]{2,1,0:T(8,128)(2,1)} %get-tuple-element.9.a, f32[320,320]{1,0:T(8,128)} %get-tuple-element.10.b, f32[320,512]{1,0:T(8,128)} %get-tuple-element.11.c), custom_call_target="tpu_custom_call" | custom-call | tf_op jit(solution)/shard_map/pallas_call | solution.py:890

commit v3 on v2

--- a/solution.py
+++ b/solution.py
@@ -98,6 +98,8 @@
     fc2_val,
     w3,
     wo,
+    w3t,
+    wot,
     f1,
     f2,
     xo,
@@ -106,6 +108,7 @@
     gb,
     tg,
     inc,
+    normed,
     own_p,
     other_p,
     pf,
@@ -216,38 +219,48 @@
     def peer(o):
         return lax.rem(ten + o, 8)
 
-    def push(name, src, slots, slot, to=None):
-        return [remote((name, o), src, slots.at[slot], device(t=peer(o))) for o in range(1, 8)]
-
-    def terms(m):
-        return r1.at[m]
-
-    def send_terms(m, rows, left_side):
-        out = []
+    def push(name, src, dst):
+        return [remote((name, o), src, dst, device(t=peer(o))) for o in range(1, 8)]
+
+    def part_rows(h):
+        return pl.ds(h * VIS, VIS)
+
+    def send_term(m, h, o):
+        j = peer(o)
+        return remote(
+            ("rs", m, h, o),
+            part.at[m, j, part_rows(h), :],
+            r1.at[m, ten, part_rows(h), :],
+            device(t=j),
+        )
+
+    def send_terms(m, product):
+        halves = 0
         for o in list(range(1, 8)) + [0]:
             j = peer(o)
-            cols = pl.ds(pl.multiple_of(j * BLK, BLK), BLK)
-            acc = nt(left_side[:, 0:256], w3[0, cols, :])
-            acc += nt(left_side[:, 256:512], w3[1, cols, :])
-            acc += nt(left_side[:, 512:768], w3[2, cols, :])
-            part[m, j, pl.ds(0, rows), :] = acc.astype(BF16)
+            acc = product(pl.ds(pl.multiple_of(j * BLK, BLK), BLK))
+            halves = acc.shape[0] // VIS
+            part[m, j, pl.ds(0, acc.shape[0]), :] = acc.astype(BF16)
             if o:
-                out.append(
-                    remote(
-                        ("rs", m, o),
-                        part.at[m, j, pl.ds(0, rows), :],
-                        r1.at[m, ten, pl.ds(0, rows), :],
-                        device(t=j),
-                    )
-                )
-        return out
-
-    def sum_terms(m, rows):
-        total = part[m, ten, pl.ds(0, rows), :].astype(F32)
+                send_term(m, 0, o)
+        for h in range(1, halves):
+            for o in range(1, 8):
+                send_term(m, h, o)
+
+    def drain_phase(halves):
+        for m in (1, 0):
+            sent_wait(("gx", m), gx_own.at[m])
+            for o in range(1, 8):
+                sent_wait(("in", m, o), ins.at[m])
+                for h in range(halves):
+                    sent_wait(("rs", m, h, o), part.at[m, peer(o), part_rows(h), :])
+
+    def sum_terms(m, h):
+        total = part[m, ten, part_rows(h), :].astype(F32)
         for o in range(1, 8):
             src = peer(8 - o)
-            ref = r1.at[m, src, pl.ds(0, rows), :]
-            arrive(("rs", m, o), ref)
+            ref = r1.at[m, src, part_rows(h), :]
+            arrive(("rs", m, h, o), ref)
             total += ref[...].astype(F32)
         return total
 
@@ -256,10 +269,9 @@
     lower = jnp.logical_not(upper)
     cut_at = 384
 
-    for m in (1, 0):
-
+    def tg_send(m):
         @pl.when(upper)
-        def _(m=m):
+        def _():
             local(("tg", m), tg_hbm.at[m, core], tg.at[m, ten])
             for o in range(1, 4):
                 remote(
@@ -277,7 +289,7 @@
                 )
 
         @pl.when(lower)
-        def _(m=m):
+        def _():
             for o in range(4):
                 remote(
                     ("tgc", m, o),
@@ -285,6 +297,8 @@
                     tg.at[m, ten, :, pl.ds(cut_at, 1024 - cut_at)],
                     device(s=1, z=1 - zl, x=lax.rem(xx + o, 4)),
                 )
+
+    tg_send(1)
 
     def tg_wait(m):
         pltpu.make_async_copy(
@@ -351,29 +365,61 @@
     sc[core] = jnp.broadcast_to(lax.rsqrt(acc / WIDTH + EPS_RMS), (SEQ, HEAD))
     sent.append(remote(("sc",), sc.at[core], sc.at[core], sibling))
 
-    lxh.wait()
-    lq.wait()
-    lkv.wait()
-    arrive(("x",), xb.at[1 - core])
-    arrive(("sc",), sc.at[1 - core])
-    arrive(("wq",), w3.at[1 - core])
-    arrive(("wkv",), w3.at[2, :, pl.ds((1 - core) * HEAD, HEAD)])
-    own_p[...] = jnp.zeros_like(own_p)
-
-    def project(i):
+    def normalize(i):
         cols = pl.ds(pl.multiple_of(i * BLK, BLK), BLK)
         rows = [
             (xb[m, :, cols].astype(F32) * sc[m][:, 0:1] * gb[i]).astype(BF16) for m in range(2)
         ]
-        normed = jnp.concatenate(rows, axis=0)
-        for j in range(3):
-            own_p[:, j * 256 : (j + 1) * 256] += nn(normed, w3[j, cols, :])
-
-    each(8, project)
-    sent.append(remote(("p",), own_p, other_p, sibling))
-
-    arrive(("p",), other_p)
-    pf[...] = own_p[...] + other_p[...]
+        normed[i] = jnp.concatenate(rows, axis=0)
+
+    def own_product(j):
+        acc = jnp.zeros((2 * SEQ, 256), F32)
+        for i in range(8):
+            acc += nn(normed[i], w3[j, i * BLK : (i + 1) * BLK, :])
+        return acc
+
+    lxh.wait()
+    arrive(("x",), xb.at[1 - core])
+    arrive(("sc",), sc.at[1 - core])
+    each(8, normalize)
+    lq.wait()
+    own_p[core] = own_product(core)
+    sent.append(remote(("p", 0), own_p.at[core], other_p.at[core], sibling))
+    tg_send(0)
+    arrive(("wq",), w3.at[1 - core])
+    own_p[1 - core] = own_product(1 - core)
+    sent.append(remote(("p", 1), own_p.at[1 - core], other_p.at[1 - core], sibling))
+    lkv.wait()
+    arrive(("wkv",), w3.at[2, :, pl.ds((1 - core) * HEAD, HEAD)])
+    own_p[2] = own_product(2)
+    sent.append(remote(("p", 2), own_p.at[2], other_p.at[2], sibling))
+
+    def head_grads(m, slots, product):
+        acc = jnp.zeros((SEQ, 512), F32)
+        for slot in slots():
+            acc += product(inc[m, slot], pl.ds(pl.multiple_of(slot * BLK, BLK), BLK))
+        gx_own[m] = acc
+        remote(("gx", m), gx_own.at[m], gx_other.at[m], sibling)
+
+    def upper_heads(m):
+        tg_wait(m)
+        flat = tg[m].reshape(8 * 48, 1024)
+        for e in range(4):
+            wide = nn(tgsel_ref[e], flat).astype(BF16)
+            inc[m, 2 * e] = wide[:, 0:BLK]
+            inc[m, 2 * e + 1] = wide[:, BLK : 2 * BLK]
+        head_grads(m, lambda: range(8), lambda block, cols: nt(block, wo[:, cols]))
+
+    lsel.wait()
+    lo.wait()
+    arrive(("wo",), wo.at[pl.ds((1 - core) * 256, 256), :])
+    pl.when(upper)(lambda: upper_heads(1))
+
+    arrive(("p", 0), other_p.at[1 - core])
+    arrive(("p", 1), other_p.at[core])
+    arrive(("p", 2), other_p.at[2])
+    for j in range(3):
+        pf[:, j * 256 : (j + 1) * 256] = own_p[j] + other_p[j]
 
     lane = lax.broadcasted_iota(jnp.int32, (SEQ, HEAD), 1)
     low = lane < 64
@@ -407,19 +453,6 @@
         top = jnp.max(scores, axis=1, keepdims=True)
         weights = jnp.where(allowed, jnp.exp(scores - top), 0.0)
         probs[m] = weights / jnp.sum(weights, axis=1, keepdims=True)
-
-    lcos.wait()
-    lsin.wait()
-    for m in (1, 0):
-        forward(m)
-
-    def head_grads(m, slots):
-        acc = jnp.zeros((SEQ, 512), F32)
-        for slot in slots():
-            cols = pl.ds(pl.multiple_of(slot * BLK, BLK), BLK)
-            acc += nt(inc[m, slot], wo[:, cols])
-        gx_own[m] = acc
-        return remote(("gx", m), gx_own.at[m], gx_other.at[m], sibling)
 
     def backward(m):
         arrive(("gx", m), gx_other.at[m])
@@ -445,10 +478,8 @@
             )
         row = to_row(inner / WIDTH)
         ins[m, :, 0:SEQ] = jnp.broadcast_to(row, (8, SEQ))
-        out = []
         for o in range(1, 8):
-            out.append(remote(("in", m, o), ins.at[m], inr.at[m, ten], device(t=peer(o))))
-        return out
+            remote(("in", m, o), ins.at[m], inr.at[m, ten], device(t=peer(o)))
 
     def inner_row(m):
         total = ins[m, 0:1, 0:SEQ]
@@ -508,27 +539,28 @@
         to = target(k)
         return (to[0] == dp) & (to[1] == pipe)
 
+    def spread_one(name, k, source, slots):
+        number = sems(name, 0) + k
+        got = recv_sem.at[sems(name, "got") + my_slot]
+
+        @pl.when(jnp.logical_not(is_self(k)))
+        def _():
+            pltpu.make_async_remote_copy(
+                src_ref=source,
+                dst_ref=slots.at[my_slot],
+                send_sem=send_sem.at[number],
+                recv_sem=got,
+                device_id=target(k),
+                device_id_type=MESH,
+            ).start()
+
+        @pl.when(is_self(k))
+        def _():
+            pltpu.make_async_copy(source, slots.at[my_slot], got).start()
+
     def spread(name, source, slots):
         for k in range(8):
-            number = sems(name, k)
-
-            def send(k=k, number=number):
-                pltpu.make_async_remote_copy(
-                    src_ref=source(k),
-                    dst_ref=slots.at[my_slot],
-                    send_sem=send_sem.at[number],
-                    recv_sem=recv_sem.at[sems(name, "got") + my_slot],
-                    device_id=target(k),
-                    device_id_type=MESH,
-                ).start()
-
-            def keep(k=k, number=number):
-                pltpu.make_async_copy(
-                    source(k), slots.at[my_slot], recv_sem.at[sems(name, "got") + my_slot]
-                ).start()
-
-            pl.when(jnp.logical_not(is_self(k)))(send)
-            pl.when(is_self(k))(keep)
+            spread_one(name, k, source(k), slots)
 
     def spread_numbers():
         for name in ("mn", "act", "gp", "vis"):
@@ -554,112 +586,165 @@
             def _(k=k, number=number):
                 pltpu.make_async_copy(source(k), source(k), send_sem.at[number]).wait()
 
+    own_cols = pl.ds(pl.multiple_of(ten * BLK, BLK), BLK)
+
+    def ga_send():
+        remote(("ga",), ga_own, ga_other, sibling)
+
+    def upper_product(m):
+        def product(cols):
+            acc = nt(acts[m, :, 0:256], w3[0, cols, :])
+            acc += nt(acts[m, :, 256:512], w3[1, cols, :])
+            return acc + nt(acts[m, :, 512:768], w3[2, cols, :])
+
+        return product
+
+    lcos.wait()
+    lsin.wait()
+    forward(1)
+
+    @pl.when(upper)
+    def _():
+        backward(1)
+        send_terms(1, upper_product(1))
+
+    forward(0)
+
     @pl.when(upper)
     def _():
         out = []
+        upper_heads(0)
+        backward(0)
+        send_terms(0, upper_product(0))
         for m in (1, 0):
-            tg_wait(m)
-            if m == 1:
-                lsel.wait()
-                lo.wait()
-                arrive(("wo",), wo.at[pl.ds((1 - core) * 256, 256), :])
-            flat = tg[m].reshape(8 * 48, 1024)
-            for e in range(4):
-                wide = nn(tgsel_ref[e], flat).astype(BF16)
-                inc[m, 2 * e] = wide[:, 0:BLK]
-                inc[m, 2 * e + 1] = wide[:, BLK : 2 * BLK]
-            out.append(head_grads(m, lambda: range(8)))
-        for m in (1, 0):
-            out.extend(backward(m))
-            out.extend(send_terms(m, SEQ, acts[m]))
-        for m in (1, 0):
-            total = sum_terms(m, SEQ)
-            inner = to_column(inner_row(m))
-            scale = sc[m][:, 0:1]
-            cols = pl.ds(pl.multiple_of(ten * BLK, BLK), BLK)
-            unit = xb[m, :, cols].astype(F32) * scale
-            w = total * gb[ten]
-            out_block[m] = (inc[m, ten].astype(F32) + scale * (w - unit * inner)).astype(BF16)
-            out.append(remote(("down", m), out_block.at[m], inc.at[m, ten], cross))
+            inner = None
+            for h in range(2):
+                total = sum_terms(m, h)
+                if h == 0:
+                    inner = to_column(inner_row(m))
+                low_row, high_row = h * VIS, (h + 1) * VIS
+                scale = sc[m, low_row:high_row, 0:1]
+                cols = pl.ds(pl.multiple_of(ten * BLK, BLK), BLK)
+                unit = xb[m, low_row:high_row, cols].astype(F32) * scale
+                w = total * gb[ten]
+                out_block[m, low_row:high_row, :] = (
+                    inc[m, ten, part_rows(h), :].astype(F32)
+                    + scale * (w - unit * inner[low_row:high_row, :])
+                ).astype(BF16)
+                out.append(
+                    remote(
+                        ("down", m, h),
+                        out_block.at[m, part_rows(h), :],
+                        inc.at[m, ten, part_rows(h), :],
+                        cross,
+                    )
+                )
         merger_forward()
         for copy in out:
             copy.wait_send()
+        drain_phase(2)
+        ga_own[...] = jnp.zeros_like(ga_own)
         for o in range(8):
-            arrive(("up", o), vis.at[peer(8 - o)])
+            slot = peer(8 - o)
+            arrive(("up", o), vis.at[slot])
+            spread_one("vis", slot, vis.at[slot], visr)
+            ga_own[...] += nt(vis[slot], f2[:, pl.ds(pl.multiple_of(slot * BLK, BLK), BLK)])
+        ga_send()
 
     @pl.when(lower)
     def _():
         merger_forward()
-        lsel.wait()
-        lo.wait()
-        arrive(("wo",), wo.at[pl.ds((1 - core) * 256, 256), :])
         out = []
         held = (1 - zl) * 4 + xx
 
-        def pass_on(m):
-            arrive(("down", m), inc.at[m, held])
-            out.extend(push(("inc", m), inc.at[m, held], inc.at[m], held))
+        def pass_on(m, h):
+            ref = inc.at[m, held, part_rows(h), :]
+            arrive(("down", m, h), ref)
+            out.extend(push(("inc", m, h), ref, ref))
 
         def blocks(m):
             yield held
             for o in range(1, 8):
-                if m == 1 and o == 5:
-                    pass_on(0)
-                src = peer(8 - o)
-                slot = lax.rem(src + 4, 8)
-                arrive((("inc", m), o), inc.at[m, slot])
+                if m == 1 and o == 4:
+                    pass_on(0, 1)
+                slot = lax.rem(peer(8 - o) + 4, 8)
+                for h in range(2):
+                    arrive((("inc", m, h), o), inc.at[m, slot, part_rows(h), :])
                 yield slot
 
-        pass_on(1)
+        def turn(i):
+            cols = pl.ds(pl.multiple_of(i * BLK, BLK), BLK)
+            wot[cols, :] = wo[:, cols].T
+            for j in range(3):
+                w3t[j, :, cols] = w3[j, cols, :].T
+
+        each(8, turn)
+        pass_on(1, 0)
+        pass_on(1, 1)
+        pass_on(0, 0)
         picks = {}
-        for m in (1, 0):
-            out.append(head_grads(m, lambda: blocks(m)))
-            out.extend(backward(m))
+
+        def pick_rows(m):
             wide = lax.broadcasted_iota(jnp.int32, (VIS, SEQ), 0) + m * VIS
             across = lax.broadcasted_iota(jnp.int32, (VIS, SEQ), 1)
             tokens = jnp.sum(jnp.where(across == wide, pos_ref[...], 0), axis=1, keepdims=True)
             picks[m] = (tokens - m * SEQ) == across
+
+        def lower_terms(m):
             pick = jnp.where(picks[m], 1.0, 0.0).astype(BF16)
-            out.extend(send_terms(m, VIS, nn(pick, acts[m]).astype(BF16)))
-        for m in (1, 0):
-            total = sum_terms(m, VIS)
+            picked = nn(pick, acts[m]).astype(BF16)
+
+            def product(cols):
+                acc = nn(picked[:, 0:256], w3t[0, :, cols])
+                acc += nn(picked[:, 256:512], w3t[1, :, cols])
+                return acc + nn(picked[:, 512:768], w3t[2, :, cols])
+
+            send_terms(m, product)
+
+        def lower_block(m):
             mask = picks[m]
             pick = jnp.where(mask, 1.0, 0.0).astype(BF16)
-            inner = jnp.sum(jnp.where(mask, inner_row(m), 0.0), axis=1, keepdims=True)
             scale_row = to_row(sc[m][:, 0:1])
             scale = jnp.sum(jnp.where(mask, scale_row, 0.0), axis=1, keepdims=True)
-            cols = pl.ds(pl.multiple_of(ten * BLK, BLK), BLK)
-            unit = nn(pick, xb[m, :, cols]) * scale
+            unit = nn(pick, xb[m, :, own_cols]) * scale
+            rows = nn(pick, inc[m, ten])
+            total = sum_terms(m, 0)
+            inner = jnp.sum(jnp.where(mask, inner_row(m), 0.0), axis=1, keepdims=True)
             w = total * gb[ten]
-            block = (nn(pick, inc[m, ten]) + scale * (w - unit * inner)).astype(BF16)
-            if m == 1:
-                out_block[0, 0:VIS, :] = block
-                for o in range(8):
-                    out.append(
-                        remote(
-                            ("up", o),
-                            out_block.at[0, pl.ds(0, VIS), :],
-                            vis.at[ten],
-                            device(s=1, t=peer(o)),
-                        )
-                    )
-            else:
-                vis[ten] = block
-                out.extend(push("visp", vis.at[ten], vis, ten))
+            return (rows + scale * (w - unit * inner)).astype(BF16)
+
+        for m in (1, 0):
+            pick_rows(m)
+            head_grads(m, lambda: blocks(m), lambda block, cols: nn(block, wot[cols, :]))
+            backward(m)
+            lower_terms(m)
+        out_block[0, 0:VIS, :] = lower_block(1)
+        for o in range(8):
+            out.append(
+                remote(
+                    ("up", o),
+                    out_block.at[0, pl.ds(0, VIS), :],
+                    vis.at[ten],
+                    device(s=1, t=peer(o)),
+                )
+            )
+        vis[ten] = lower_block(0)
+        out.extend(push("visp", vis.at[ten], vis.at[ten]))
+        spread_one("vis", ten, vis.at[ten], visr)
+        ga_own[...] = nt(vis[ten], f2[:, own_cols])
         for o in range(1, 8):
-            arrive(("visp", o), vis.at[peer(8 - o)])
+            slot = peer(8 - o)
+            arrive(("visp", o), vis.at[slot])
+            spread_one("vis", slot, vis.at[slot], visr)
+            ga_own[...] += nt(vis[slot], f2[:, pl.ds(pl.multiple_of(slot * BLK, BLK), BLK)])
+        ga_send()
         for copy in out:
             copy.wait_send()
-
-    spread("vis", lambda k: vis.at[k], visr)
-    ga_own[...] = jnp.zeros_like(ga_own)
-    for i in range(8):
-        ga_own[...] += nt(vis[i], f2[:, i * BLK : (i + 1) * BLK])
-    sent.append(remote(("ga",), ga_own, ga_other, sibling))
+        drain_phase(1)
+
     arrive(("ga",), ga_other)
     grad_pre = ((ga_own[...] + ga_other[...]) * slope[...]).astype(BF16)
     gpre[:, 0:PIECE] = grad_pre
-    spread("gp", lambda k: gpre, gpr)
     stat_lane = lax.broadcasted_iota(jnp.int32, (VIS, LANES - PIECE), 1)
     for q in range(2):
         cols = pl.ds(pl.multiple_of(core * 2 * CTX + q * CTX, CTX), CTX)
@@ -685,13 +770,7 @@
     for o in range(1, 8):
         to = lax.rem(ten + o, 8)
         sent.append(remote(("pg", o), pgp.at[to], pgpr.at[ten], device(t=to)))
-
-    collect("act", actr)
-    collect("vis", visr)
-    fc2_val[...] = tn(
-        actr[...].reshape(8 * VIS, LANES)[:, 0:PIECE], visr[...].reshape(8 * VIS, BLK)
-    )
-    out2 = local("fc2", fc2_val, fc2_out)
+    spread("gp", lambda k: gpre, gpr)
 
     total = pgp[ten].astype(F32)
     for o in range(1, 8):
@@ -722,6 +801,12 @@
         )
     pgr[my_code] = pgs[core]
 
+    collect("act", actr)
+    collect("vis", visr)
+    fc2_val[...] = tn(
+        actr[...].reshape(8 * VIS, LANES)[:, 0:PIECE], visr[...].reshape(8 * VIS, BLK)
+    )
+    out2 = local("fc2", fc2_val, fc2_out)
     collect("mn", mnr)
     collect("gp", gpr)
     fc1_val[...] = tn(
@@ -745,6 +830,7 @@
     out1.wait()
     out2.wait()
     tg_drain()
+    sent_wait(("ga",), ga_own)
     sent_wait(("pu",), pu.at[core])
     sent_wait(("iv",), iv.at[core])
     drain_spread("mn", lambda k: mns.at[8 * core + k])
@@ -817,6 +903,8 @@
             v((PIECE, BLK), F32),
             v((3, HALF, 256), BF16),
             v((512, HALF), BF16),
+            v((3, 256, HALF), BF16),
+            v((HALF, 512), BF16),
             v((PIECE, 4 * CTX), BF16),
             v((PIECE, HALF), BF16),
             v((SEQ, WIDTH), BF16),
@@ -825,8 +913,9 @@
             v((8, 1, BLK), F32),
             v((2, 8, 48, 1024), BF16),
             v((2, 8, SEQ, BLK), BF16),
-            v((2 * SEQ, 768), F32),
-            v((2 * SEQ, 768), F32),
+            v((8, 2 * SEQ, BLK), BF16),
+            v((3, 2 * SEQ, 256), F32),
+            v((3, 2 * SEQ, 256), F32),
             v((2 * SEQ, 768), F32),
             v((2, 4 * SEQ, HEAD), BF16),
             v((2, SEQ, HEAD), BF16),
@@ -860,8 +949,8 @@
             v((8, VIS, LANES), BF16),
             v((2, 16, BLK), BF16),
             v((16, 16, BLK), BF16),
-            pltpu.SemaphoreType.DMA((224,)),
-            pltpu.SemaphoreType.DMA((224,)),
+            pltpu.SemaphoreType.DMA((288,)),
+            pltpu.SemaphoreType.DMA((288,)),
             pltpu.SemaphoreType.DMA((20,)),
             pltpu.SemaphoreType.REGULAR((2,)),
         ],

time: 115 us -> 107 us (0.930); the launches traced: 115 us -> 106 us
  Pallas kernels: 112 us -> 103 us
    pallas_call x1, Pallas kernels: 110 us -> 100 us  [local(): pl.pallas_call(kernel, out_shape=(jax.ShapeDtypeStruct((1, 24, 4 * CTX),...]
where the time goes in v3:
time: 107 us; the launch traced here: 106 us
  Pallas kernels  103 us (96%)
  local copies, waits for them, and re-layouts  2.38 us (2%)
    pallas_call x1, Pallas kernels, local(): pl.pallas_call(kernel, out_shape=(jax.ShapeDtypeStruct((1, 24, 4 * CTX),...  100 us
    pallas_call x1, Pallas kernels, local(): pl.pallas_call(hand_over, out_shape=tuple((jax.ShapeDtypeStruct(a.shape,...  2.47 us

profile of v3, /device:TPU:1, one launch (start us, length us, event | category | flops | bytes accessed | tf_op | source)
XLA Modules:
  0.0 105.9 jit_solution(404069065043631234)
XLA Ops:
  0.6 1.2 %reshape_squeeze.3 = bf16[2,12,2,4,1024]{4,3,2,0,1:T(4,128)(2,1)S(1)} reshape(bf16[1,2,12,8192]{3,1,2,0:T(2,128)(2,1)} %param.18) | data formatting | bytes 786432 | tf_op jit(solution)/shard_map/reshape;squeeze | solution.py:881
  1.9 0.3 copy.21
  2.2 0.8 copy.22.tg_hbm
  3.0 100.4 %shard_map.184 = (bf16[1,24,5120]{2,1,0:T(8,128)(2,1)}, f32[320,320]{1,0:T(8,128)}, f32[320,512]{1,0:T(8,128)}) custom-call(bf16[96,8192]{1,0:T(8,128)(2,1)} %bitcast.15, bf16[2,2,48,1024]{3,2,1,0:T(8,128)(2,1)} %copy.22.tg_hbm, f32[2,8192]{1,0:T(2,128)} %gain_ref.1, bf16[8192,256]{1,0:T(8,128)(2,1)} %bitcast.11, bf16[8192,128]{1,0:T(8,128)(2,1)} %bitcast.14, ...), custom_call_target="tpu_custom_call" | custom-call | tf_op jit(solution)/shard_map/pallas_call | solution.py:886
  103.4 2.5 %shard_map.185 = (bf16[1,24,5120]{2,1,0:T(8,128)(2,1)}, f32[320,320]{1,0:T(8,128)}, f32[320,512]{1,0:T(8,128)}) custom-call(bf16[1,24,5120]{2,1,0:T(8,128)(2,1)} %get-tuple-element.9.a, f32[320,320]{1,0:T(8,128)} %get-tuple-element.10.b, f32[320,512]{1,0:T(8,128)} %get-tuple-element.11.c), custom_call_target="tpu_custom_call" | custom-call | tf_op jit(solution)/shard_map/pallas_call | solution.py:979

commit v4 on v3

--- a/solution.py
+++ b/solution.py
@@ -738,9 +738,6 @@
             spread_one("vis", slot, vis.at[slot], visr)
             ga_own[...] += nt(vis[slot], f2[:, pl.ds(pl.multiple_of(slot * BLK, BLK), BLK)])
         ga_send()
-        for copy in out:
-            copy.wait_send()
-        drain_phase(1)
 
     arrive(("ga",), ga_other)
     grad_pre = ((ga_own[...] + ga_other[...]) * slope[...]).astype(BF16)
@@ -791,13 +788,11 @@
     my_code = core * 8 + ten
     for o in range(1, 16):
         code = lax.rem(my_code + o, 16)
-        sent.append(
-            remote(
-                ("po", o),
-                pgs.at[code // 8],
-                pgr.at[my_code],
-                device(b=code // 8, t=lax.rem(code, 8)),
-            )
+        remote(
+            ("po", o),
+            pgs.at[code // 8],
+            pgr.at[my_code],
+            device(b=code // 8, t=lax.rem(code, 8)),
         )
     pgr[my_code] = pgs[core]
 
@@ -813,6 +808,30 @@
         mnr[...].reshape(8 * VIS, LANES)[:, 0:PIECE], gpr[...].reshape(8 * VIS, LANES)[:, 0:PIECE]
     )
     out1 = local("fc1", fc1_val, fc1_out)
+
+    @pl.when(lower)
+    def _():
+        held = (1 - zl) * 4 + xx
+        for m in range(2):
+            for h in range(2):
+                for o in range(1, 8):
+                    sent_wait((("inc", m, h), o), inc.at[m, held, part_rows(h), :])
+        for o in range(8):
+            sent_wait(("up", o), out_block.at[0, pl.ds(0, VIS), :])
+        for o in range(1, 8):
+            sent_wait(("visp", o), vis.at[ten])
+        drain_phase(1)
+
+    for copy in sent:
+        copy.wait_send()
+    tg_drain()
+    sent_wait(("ga",), ga_own)
+    sent_wait(("pu",), pu.at[core])
+    sent_wait(("iv",), iv.at[core])
+    drain_spread("mn", lambda k: mns.at[8 * core + k])
+    drain_spread("act", lambda k: act)
+    drain_spread("gp", lambda k: gpre)
+    drain_spread("vis", lambda k: vis.at[k])
     for o in range(1, 16):
         arrive(("po", o), pgr.at[lax.rem(my_code + 16 - o, 16)])
     for q in range(4):
@@ -825,18 +844,10 @@
             pieces.append(jnp.concatenate([msg[:, 0:PIECE], tail], axis=0))
         pg_out[0, :, q * CTX : (q + 1) * CTX] = jnp.concatenate(pieces, axis=1).astype(BF16)
 
-    for copy in sent:
-        copy.wait_send()
+    for b_code in range(1, 16):
+        sent_wait(("po", b_code), pgs.at[core])
     out1.wait()
     out2.wait()
-    tg_drain()
-    sent_wait(("ga",), ga_own)
-    sent_wait(("pu",), pu.at[core])
-    sent_wait(("iv",), iv.at[core])
-    drain_spread("mn", lambda k: mns.at[8 * core + k])
-    drain_spread("act", lambda k: act)
-    drain_spread("gp", lambda k: gpre)
-    drain_spread("vis", lambda k: vis.at[k])
 
 
 def hand_over(a, b, c, a_out, b_out, c_out):

time: 107 us -> 106 us (level)
  no operation moved by 1% of the time
where the time goes in v4:
time: 106 us
  Pallas kernels  103 us (97%)
  local copies, waits for them, and re-layouts  2.38 us (2%)
    pallas_call x1, Pallas kernels, local(): pl.pallas_call(kernel, out_shape=(jax.ShapeDtypeStruct((1, 24, 4 * CTX),...  100 us
    pallas_call x1, Pallas kernels, local(): pl.pallas_call(hand_over, out_shape=tuple((jax.ShapeDtypeStruct(a.shape,...  2.47 us

profile of v4, /device:TPU:1, one launch (start us, length us, event | category | flops | bytes accessed | tf_op | source)
XLA Modules:
  0.0 105.8 jit_solution(14708899730813976018)
XLA Ops:
  0.6 1.2 %reshape_squeeze.3 = bf16[2,12,2,4,1024]{4,3,2,0,1:T(4,128)(2,1)S(1)} reshape(bf16[1,2,12,8192]{3,1,2,0:T(2,128)(2,1)} %param.18) | data formatting | bytes 786432 | tf_op jit(solution)/shard_map/reshape;squeeze | solution.py:892
  1.9 0.3 copy.21
  2.2 0.8 copy.22.tg_hbm
  3.0 100.3 %shard_map.184 = (bf16[1,24,5120]{2,1,0:T(8,128)(2,1)}, f32[320,320]{1,0:T(8,128)}, f32[320,512]{1,0:T(8,128)}) custom-call(bf16[96,8192]{1,0:T(8,128)(2,1)} %bitcast.15, bf16[2,2,48,1024]{3,2,1,0:T(8,128)(2,1)} %copy.22.tg_hbm, f32[2,8192]{1,0:T(2,128)} %gain_ref.1, bf16[8192,256]{1,0:T(8,128)(2,1)} %bitcast.11, bf16[8192,128]{1,0:T(8,128)(2,1)} %bitcast.14, ...), custom_call_target="tpu_custom_call" | custom-call | tf_op jit(solution)/shard_map/pallas_call | solution.py:897
  103.3 2.5 %shard_map.185 = (bf16[1,24,5120]{2,1,0:T(8,128)(2,1)}, f32[320,320]{1,0:T(8,128)}, f32[320,512]{1,0:T(8,128)}) custom-call(bf16[1,24,5120]{2,1,0:T(8,128)(2,1)} %get-tuple-element.9.a, f32[320,320]{1,0:T(8,128)} %get-tuple-element.10.b, f32[320,512]{1,0:T(8,128)} %get-tuple-element.11.c), custom_call_target="tpu_custom_call" | custom-call | tf_op jit(solution)/shard_map/pallas_call | solution.py:990

commit v5 on v3

--- a/solution.py
+++ b/solution.py
@@ -172,9 +172,10 @@
     barrier = pltpu.get_barrier_semaphore()
     up_y = device(d=lax.rem(dp + 1, 4))
     down_y = device(d=lax.rem(dp + 3, 4))
-    greeted = [sibling, up_y, down_y, device(s=1 - phase)]
-    greeted += [device(t=lax.rem(ten + o, 8)) for o in range(1, 8)]
-    greeted += [device(s=1 - phase, z=1 - zl, x=lax.rem(xx + o, 4)) for o in range(4)]
+    greeted = [device(s=1 - phase, z=1 - zl, x=lax.rem(xx + 4 - o, 4)) for o in range(1, 5)]
+    greeted += [device(s=1 - phase)]
+    greeted += [device(t=lax.rem(ten + 8 - o, 8)) for o in range(1, 8)]
+    greeted += [up_y, down_y, sibling]
     for to in greeted:
         pl.semaphore_signal(barrier, inc=1, device_id=to, device_id_type=MESH)
 
@@ -853,7 +854,7 @@
     for e in range(4):
         for t in range(8):
             for i in range(12):
-                pick[e, t * 12 + i, t * 48 + e * 12 + i] = 1.0
+                pick[e, t * 12 + i, t * 48 + i * 4 + e] = 1.0
     return (
         np.concatenate([cosine, cosine], axis=1).astype(np.float32),
         np.concatenate([-sine, sine], axis=1).astype(np.float32),
@@ -878,7 +879,7 @@
     fc2_weight,
 ):
     cosine, sine, pick = tables()
-    shards = top_grad[0].reshape(2, 12, 2, 4, 1024).transpose(0, 2, 3, 1, 4)
+    shards = top_grad[0].reshape(2, 12, 2, HALF).transpose(0, 2, 1, 3)
     shards = shards.reshape(2, 2, 48, 1024)
     vmem = pl.BlockSpec(memory_space=pltpu.VMEM)
     hbm = pl.BlockSpec(memory_space=pl.ANY)

time: 107 us -> 107 us (level)
  no operation moved by 1% of the time
where the time goes in v5:
time: 107 us; the launch traced here: 106 us
  Pallas kernels  103 us (96%)
  local copies, waits for them, and re-layouts  2.52 us (2%)
    pallas_call x1, Pallas kernels, local(): pl.pallas_call(kernel, out_shape=(jax.ShapeDtypeStruct((1, 24, 4 * CTX),...  100 us
    pallas_call x1, Pallas kernels, local(): pl.pallas_call(hand_over, out_shape=tuple((jax.ShapeDtypeStruct(a.shape,...  2.47 us

profile of v5, /device:TPU:1, one launch (start us, length us, event | category | flops | bytes accessed | tf_op | source)
XLA Modules:
  0.0 106.0 jit_solution(10947210996802637371)
XLA Ops:
  0.6 1.3 %reshape_squeeze.3 = bf16[2,12,2,4096]{3,2,0,1:T(2,128)(2,1)S(1)} reshape(bf16[1,2,12,8192]{3,1,2,0:T(2,128)(2,1)} %param.18) | data formatting | bytes 786432 | tf_op jit(solution)/shard_map/reshape;squeeze | solution.py:882
  1.9 0.2 copy.23
  2.2 1.0 reshape.18.tg_hbm
  3.2 100.3 %shard_map.184 = (bf16[1,24,5120]{2,1,0:T(8,128)(2,1)}, f32[320,320]{1,0:T(8,128)}, f32[320,512]{1,0:T(8,128)}) custom-call(bf16[96,8192]{1,0:T(8,128)(2,1)} %bitcast.16, bf16[2,2,48,1024]{3,2,1,0:T(8,128)(2,1)} %reshape.18.tg_hbm, f32[2,8192]{1,0:T(2,128)} %gain_ref.1, bf16[8192,256]{1,0:T(8,128)(2,1)} %bitcast.11, bf16[8192,128]{1,0:T(8,128)(2,1)} %bitcast.14, ...), custom_call_target="tpu_custom_call" | custom-call | tf_op jit(solution)/shard_map/pallas_call | solution.py:887
  103.5 2.5 %shard_map.185 = (bf16[1,24,5120]{2,1,0:T(8,128)(2,1)}, f32[320,320]{1,0:T(8,128)}, f32[320,512]{1,0:T(8,128)}) custom-call(bf16[1,24,5120]{2,1,0:T(8,128)(2,1)} %get-tuple-element.9.a, f32[320,320]{1,0:T(8,128)} %get-tuple-element.10.b, f32[320,512]{1,0:T(8,128)} %get-tuple-element.11.c), custom_call_target="tpu_custom_call" | custom-call | tf_op jit(solution)/shard_map/pallas_call | solution.py:980
